TPU v7x, 32 devices: a whole 2x2x4 slice. The times are simulated.
32 devices in a mesh: panel: 8 (over y, x, core), group: 4 (over z).
Axes of the slice: x: 2, y: 2, z: 4, core: 2. Of those that a mesh axis runs over, the one named last changes fastest.
Arguments:
- displacement: bfloat16 [96, 524288], P(None, ('panel', 'group')), may hold values from -6 to 6
- send_index: int32 [32, 16384], P(('panel', 'group')), may hold values from 0 to 16383, each once within a row
- support: int32 [32, 16384], P(('panel', 'group')), may hold values from 0 to 16383, each once within a row
- support_xyz: float32 [3, 524288], P(None, ('panel', 'group')), may hold values from -1.1 to 1.1, as said below
- patch_kernel_inverse: bfloat16 [64, 64, 8192], P('group', None, 'panel'), may hold values from -0.75 to 0.75
- panel_xyz: float32 [3, 65536], P(None, ('panel', 'group')), may hold values from -1.1 to 1.1, as said below
- normals: float32 [3, 65536], P(None, ('panel', 'group')), may hold values from -3 to 3
- centers: float32 [3, 8192], P(None, ('panel', 'group')), may hold values from -1 to 1
- member: int32 [65536], P(('panel', 'group')), may hold values from 0 to 255
Outputs:
- normal_velocity: float32 [32, 65536], P(None, ('panel', 'group'))
Inputs may be any that keep to these rules, and one draw needn't show every extreme that they name: `send_index`: each row is a permutation: every local node of a window is sent to exactly one slot. `support`: each row is a permutation: every received slot of a window is used by exactly one patch entry. `support_xyz`: each coordinate lies within 0.1 of its patch's centre. `panel_xyz`: each coordinate lies within 0.1 of its home patch's centre.
All inputs are finite; a program needn't handle non-finite values.
Results may differ from a plain program's by a relative error of at most 0.005.
Values may be sent and summed in bfloat16 or wider, within the bound.
No kernel may reach another device: no remote copies, remote signals or barrier semaphores. Data moves between devices by JAX's collectives and lax.ppermute only.
A program may use at most 192 MiB of HBM per device.

v0:
```python
import jax
import jax.numpy as jnp
from jax import lax
from jax.sharding import PartitionSpec as P

KERNEL_RADIUS = 0.45
ATTRACTION_REACH = 0.3
OWNER_PREMIUM = 8.0


def compact_kernel(scaled):
    falloff = jnp.maximum(1.0 - scaled, 0.0)
    return falloff**4 * (4.0 * scaled + 1.0)


def blend_patch_major(points, member, support_xyz, centers, support_count):
    dist_sq = (points[0][:, None] - support_xyz[0][None, :]) ** 2
    dist_sq = dist_sq + (points[1][:, None] - support_xyz[1][None, :]) ** 2
    dist_sq = dist_sq + (points[2][:, None] - support_xyz[2][None, :]) ** 2
    kernel = compact_kernel(jnp.sqrt(dist_sq) / KERNEL_RADIUS)
    center_distance_squared = (points[0][:, None] - centers[0][None, :]) ** 2
    center_distance_squared = (
        center_distance_squared + (points[1][:, None] - centers[1][None, :]) ** 2
    )
    center_distance_squared = (
        center_distance_squared + (points[2][:, None] - centers[2][None, :]) ** 2
    )
    patches = centers.shape[1]
    owner_patch = member[:, None] == jnp.arange(patches, dtype=jnp.int32)[None, :]
    patch_attraction = compact_kernel(
        jnp.sqrt(center_distance_squared) / ATTRACTION_REACH
    ) + jnp.where(owner_patch, OWNER_PREMIUM, 0.0)
    weights = patch_attraction / jnp.sum(patch_attraction, axis=1, keepdims=True)
    rows = points.shape[1]
    blended = kernel.reshape(rows, patches, support_count) * weights[:, :, None]
    return blended.astype(jnp.bfloat16).reshape(rows, patches * support_count)


def patch_products(inverse, values):
    return jnp.einsum("jkp,cpk->cpj", inverse, values, preferred_element_type=jnp.float32)


def shards(
    displacement,
    send_index,
    support,
    support_xyz,
    patch_kernel_inverse,
    panel_xyz,
    normals,
    centers,
    member,
):
    columns = displacement.shape[0]
    modes = columns // 3
    slots = send_index.shape[1]
    patches = centers.shape[1]
    support_count = slots // patches
    outgoing = jnp.take(displacement, send_index[0], axis=1)
    arriving_rows = lax.all_to_all(
        outgoing, ("panel", "group"), split_axis=1, concat_axis=1, tiled=True
    )
    values = jnp.take(arriving_rows, support[0], axis=1).reshape(columns, patches, support_count)
    own_inverse = lax.all_to_all(
        patch_kernel_inverse, "group", split_axis=2, concat_axis=0, tiled=True
    )
    coefficient = patch_products(own_inverse, values).astype(jnp.bfloat16)
    flat = coefficient.reshape(columns, slots)
    panels = panel_xyz.shape[1]
    block_rows = min(512, panels)
    pieces = []
    for offset in range(0, panels, block_rows):
        points = panel_xyz[:, offset : offset + block_rows]
        blend = blend_patch_major(
            points, member[offset : offset + block_rows], support_xyz, centers, support_count
        )
        moved = jnp.einsum("cs,ns->cn", flat, blend, preferred_element_type=jnp.float32)
        moved = moved.reshape(3, modes, block_rows)
        facing = normals[:, offset : offset + block_rows]
        pieces.append(jnp.sum(moved * facing[:, None, :], axis=0))
    return jnp.concatenate(pieces, axis=1)


def solution(mesh):
    return jax.shard_map(
        shards,
        mesh=mesh,
        in_specs=(
            P(None, ("panel", "group")),
            P(("panel", "group"), None),
            P(("panel", "group"), None),
            P(None, ("panel", "group")),
            P("group", None, "panel"),
            P(None, ("panel", "group")),
            P(None, ("panel", "group")),
            P(None, ("panel", "group")),
            P(("panel", "group")),
        ),
        out_specs=P(None, ("panel", "group")),
        check_vma=False,
    )
```

profile of v0, /device:TPU:0, one launch (start us, length us, event | category | flops | bytes accessed | tf_op | source)
XLA Modules:
  0.0 365.7 jit_solution(16847969331953554416)
XLA Ops:
  0.0 6.2 %copy.26 = bf16[16,64,1024]{1,0,2:T(8,128)(2,1)} copy(bf16[16,64,1024]{2,1,0:T(8,128)(2,1)} %param.15) | data formatting | bytes 4194304 | tf_op args[4]
  6.2 5.9 %reshape.1307 = bf16[4,2,131072]{2,1,0:T(2,128)(2,1)} reshape(bf16[1024,16,64]{2,1,0:T(8,128)(2,1)} %bitcast.64) | data formatting | bytes 4194304
  12.1 6.3 %all-to-all-start.1 = ((bf16[4,2,131072]{2,1,0:T(2,128)(2,1)}), bf16[4,2,131072]{2,1,0:T(2,128)(2,1)S(1)}, u32[]{:S(2)}, u32[]{:S(2)}) async-start(bf16[4,2,131072]{2,1,0:T(2,128)(2,1)} %reshape.1307), calls=%async_computation.1 | async-start | bytes 4194304 | tf_op jit(solution)/shard_map/all_to_all | solution.py:64
  18.4 0.0 copy-done.1
  18.5 5.9 %copy.23 = bf16[96,16384]{0,1:T(8,128)(2,1)} copy(bf16[96,16384]{1,0:T(8,128)(2,1)} %param.11) | data formatting | bytes 6291456 | tf_op args[0]
  24.4 57.7 %gather_fusion = bf16[16384,96]{1,0:T(8,128)(2,1)} fusion(bf16[96,16384]{0,1:T(8,128)(2,1)} %copy.23, s32[16384]{0:T(1024)S(1)} %fusion.8), kind=kCustom, calls=%fused_computation.clone | custom fusion | bytes 6356992 | tf_op jit(solution)/shard_map/jit(_take)/gather | solution.py:59
  82.1 11.5 %broadcast_select_fusion.1 = bf16[16384,96]{1,0:T(8,128)(2,1)} fusion(bf16[16384,96]{1,0:T(8,128)(2,1)} %gather_fusion, pred[16384]{0:T(1024)(128)(4,1)S(1)} %compare_and_fusion.1), kind=kLoop, calls=%fused_computation.8 | loop fusion | flops 1572864 | bytes 6307840 | tf_op jit(solution)/shard_map/jit(_take)/select_n | solution.py:59
  93.7 6.2 %copy.24 = bf16[96,32,512]{2,0,1:T(8,128)(2,1)} copy(bf16[96,32,512]{0,2,1:T(8,128)(2,1)} %bitcast.63) | data formatting | bytes 6291456 | tf_op jit(solution)/shard_map/all_to_all | solution.py:60
  99.9 0.0 copy-done.3
  99.9 0.5 slice_reduce_fusion.2
  100.4 0.1 sub.556
  100.5 0.1 sub.551
  100.6 0.1 sub.546
  100.7 0.0 copy-done.15
  100.7 0.0 copy-done.14
  100.7 0.0 copy-done.13
  100.8 0.0 copy-start.5
  100.8 0.0 copy-start.6
  100.8 0.0 copy-start.7
  100.8 0.0 copy-start.8
  100.8 0.0 copy-start.9
  100.8 2.0 fusion.4
  102.8 1.3 broadcast_divide_fusion.2
  104.2 2.6 broadcast_divide_fusion.3
  106.8 0.0 all-to-all-done.1
  106.9 1.2 copy-done
  108.1 6.2 %all-to-all-start = ((bf16[96,32,512]{2,0,1:T(8,128)(2,1)}), bf16[96,32,512]{2,0,1:T(8,128)(2,1)S(1)}, u32[]{:S(2)}, u32[]{:S(2)}) async-start(bf16[96,32,512]{2,0,1:T(8,128)(2,1)} %copy.24), calls=%async_computation | async-start | bytes 6291456 | tf_op jit(solution)/shard_map/all_to_all | solution.py:60
  114.4 0.0 copy-start.4
  114.4 0.0 copy-start.2
  114.4 113.5 %multiply_convert_fusion.3 = (bf16[512,256,64]{0,2,1:T(8,128)(2,1)}, bf16[512,256,64]{0,2,1:T(8,128)(2,1)}, bf16[512,256,64]{0,2,1:T(8,128)(2,1)}, bf16[512,256,64]{0,2,1:T(8,128)(2,1)}) fusion(f32[512,256]{0,1:T(8,128)} %get-tuple-element.40, f32[256,64]{1,0:T(8,128)S(1)} %sub.556, f32[512]{0:T(512)} %bitcast.93, f32[256,64]{1,0:T(8,128)S(1)} %sub.551, ...), kind=kLoop, calls=%fused_computation.5 | loop fusion | flops 603979776 | bytes 69427200 | tf_op jit(solution)/shard_map/convert_element_type | solution.py:36
  228.0 5.8 %reshape.1308 = bf16[1024,16,64]{2,1,0:T(8,128)(2,1)} reshape(bf16[4,2,131072]{2,1,0:T(2,128)(2,1)} %copy-done) | data formatting | bytes 4194304
  233.9 5.5 %copy.27 = bf16[16,64,4,256]{1,0,2,3:T(8,128)(2,1)} copy(bf16[16,64,4,256]{1,0,3,2:T(8,128)(2,1)} %bitcast.65) | data formatting | bytes 4194304 | tf_op jit(solution)/shard_map/all_to_all | solution.py:64
  239.4 0.0 all-to-all-done
  239.4 4.3 %copy.25 = bf16[96,32,512]{0,2,1:T(8,128)(2,1)} copy(bf16[96,32,512]{2,0,1:T(8,128)(2,1)S(1)} %all-to-all-done) | data formatting | bytes 6291456 | tf_op jit(solution)/shard_map/all_to_all | solution.py:60
  243.6 57.7 %gather_fusion.1 = bf16[16384,96]{1,0:T(8,128)(2,1)} fusion(bf16[96,16384]{0,1:T(8,128)(2,1)} %bitcast.54, s32[16384]{0:T(1024)S(1)} %fusion.9), kind=kCustom, calls=%fused_computation.1.clone | custom fusion | bytes 6356992 | tf_op jit(solution)/shard_map/jit(_take)/gather | solution.py:63
  301.3 10.9 %broadcast_select_fusion = bf16[16384,96]{1,0:T(8,128)(2,1)S(1)} fusion(bf16[16384,96]{1,0:T(8,128)(2,1)} %gather_fusion.1, pred[16384]{0:T(1024)(128)(4,1)S(1)} %compare_and_fusion), kind=kLoop, calls=%fused_computation.7 | loop fusion | flops 1572864 | bytes 6307840 | tf_op jit(solution)/shard_map/jit(_take)/select_n | solution.py:63
  312.3 5.4 %convert_bitcast_fusion = bf16[96,256,64]{0,2,1:T(8,128)(2,1)} fusion(bf16[64,64,256]{1,0,2:T(8,128)(2,1)} %bitcast.61, bf16[96,256,64]{0,2,1:T(8,128)(2,1)S(1)} %bitcast.62), kind=kOutput, calls=%fused_computation.6 | convolution fusion | flops 202899456 | bytes 8388608 | tf_op jit(solution)/shard_map/jkp,cpk->cpj/dot_general | solution.py:40
  317.7 11.2 %copy.28 = bf16[96,256,64]{2,1,0:T(8,128)(2,1)} copy(bf16[96,256,64]{0,2,1:T(8,128)(2,1)} %convert_bitcast_fusion) | data formatting | bytes 6291456 | tf_op jit(solution)/shard_map/convert_element_type | solution.py:67
  329.0 7.3 %dot_general.18 = bf16[3,32,16384]{2,1,0:T(8,128)(2,1)S(1)} reshape(bf16[96,256,64]{2,1,0:T(8,128)(2,1)} %copy.28) | data formatting | bytes 6291456 | tf_op jit(solution)/shard_map/cs,ns->cn/dot_general | solution.py:77
  336.2 8.5 %fusion.3 = f32[32,512]{1,0:T(8,128)S(1)} fusion(bf16[3,32,16384]{2,1,0:T(8,128)(2,1)S(1)} %dot_general.18, bf16[512,16384,1]{0,1,2:T(8,128)(2,1)} %bitcast.60, f32[3,512]{1,0:T(4,128)S(1)} %get-tuple-element.19), kind=kOutput, calls=%fused_computation.16 | convolution fusion | flops 1610694656 | bytes 19994624 | tf_op jit(solution)/shard_map/cs,ns->cn/dot_general | solution.py:77
  344.8 0.0 slice-start
  344.8 0.0 slice-start.1
  344.8 8.7 %fusion.2 = f32[32,512]{1,0:T(8,128)S(1)} fusion(bf16[3,32,16384]{2,1,0:T(8,128)(2,1)S(1)} %dot_general.18, bf16[512,16384,1]{0,1,2:T(8,128)(2,1)} %bitcast.59, f32[3,512]{1,0:T(4,128)S(1)} %get-tuple-element.20), kind=kOutput, calls=%fused_computation.15 | convolution fusion | flops 1610694656 | bytes 19994624 | tf_op jit(solution)/shard_map/cs,ns->cn/dot_general | solution.py:77
  353.5 0.0 slice-start.2
  353.5 0.0 slice-start.3
  353.5 8.7 %fusion.1 = f32[32,512]{1,0:T(8,128)S(1)} fusion(bf16[3,32,16384]{2,1,0:T(8,128)(2,1)S(1)} %dot_general.18, bf16[512,16384,1]{0,1,2:T(8,128)(2,1)} %bitcast.58, f32[3,512]{1,0:T(4,128)S(1)} %get-tuple-element.18), kind=kOutput, calls=%fused_computation.14 | convolution fusion | flops 1610694656 | bytes 19994624 | tf_op jit(solution)/shard_map/cs,ns->cn/dot_general | solution.py:77
  362.2 2.8 fusion
  365.0 0.7 pad_maximum_fusion
  (32 shorter events, 0.2 us)
Async XLA Ops:
  0.0 18.4 %copy-start.1 = (s32[1,16384]{1,0:T(1,128)S(1)}, s32[1,16384]{1,0:T(1,128)}, u32[]{:S(2)}) copy-start(s32[1,16384]{1,0:T(1,128)} %param.12) | copy-start | bytes 196612
  12.1 94.7 %all-to-all-start.1 = ((bf16[4,2,131072]{2,1,0:T(2,128)(2,1)}), bf16[4,2,131072]{2,1,0:T(2,128)(2,1)S(1)}, u32[]{:S(2)}, u32[]{:S(2)}) async-start(bf16[4,2,131072]{2,1,0:T(2,128)(2,1)} %reshape.1307), calls=%async_computation.1 | async-start | bytes 4194304 | tf_op jit(solution)/shard_map/all_to_all | solution.py:64
  24.4 75.5 %copy-start.3 = (f32[3,16384]{1,0:T(4,128)S(1)}, f32[3,16384]{1,0:T(4,128)}, u32[]{:S(2)}) copy-start(f32[3,16384]{1,0:T(4,128)} %param.14) | copy-start | bytes 589828
  24.4 76.3 %copy-start.15 = (f32[3,256]{1,0:T(4,128)S(1)}, f32[3,256]{1,0:T(4,128)}, u32[]{:S(2)}) copy-start(f32[3,256]{1,0:T(4,128)} %param.18) | copy-start | bytes 9220
  24.4 76.3 %copy-start.14 = (s32[2048]{0:T(1024)S(1)}, s32[2048]{0:T(1024)}, u32[]{:S(2)}) copy-start(s32[2048]{0:T(1024)} %param.19) | copy-start | bytes 24580
  24.4 76.3 %copy-start.13 = (f32[3,2048]{1,0:T(4,128)S(1)}, f32[3,2048]{1,0:T(4,128)}, u32[]{:S(2)}) copy-start(f32[3,2048]{1,0:T(4,128)} %param.16) | copy-start | bytes 73732
  100.8 6.0 %copy-start.5 = (f32[1,512]{1,0:T(1,128)}, f32[1,512]{1,0:T(1,128)S(1)}, u32[]{:S(2)}) copy-start(f32[1,512]{1,0:T(1,128)S(1)} %get-tuple-element.25) | copy-start | bytes 6148
  100.8 6.0 %copy-start.6 = (f32[1,512]{1,0:T(1,128)}, f32[1,512]{1,0:T(1,128)S(1)}, u32[]{:S(2)}) copy-start(f32[1,512]{1,0:T(1,128)S(1)} %get-tuple-element.26) | copy-start | bytes 6148
  100.8 6.0 %copy-start.7 = (f32[1,512]{1,0:T(1,128)}, f32[1,512]{1,0:T(1,128)S(1)}, u32[]{:S(2)}) copy-start(f32[1,512]{1,0:T(1,128)S(1)} %get-tuple-element.27) | copy-start | bytes 6148
  100.8 6.0 %copy-start.8 = (f32[1,512]{1,0:T(1,128)}, f32[1,512]{1,0:T(1,128)S(1)}, u32[]{:S(2)}) copy-start(f32[1,512]{1,0:T(1,128)S(1)} %get-tuple-element.28) | copy-start | bytes 6148
  100.8 6.0 %copy-start.9 = (f32[1,512]{1,0:T(1,128)}, f32[1,512]{1,0:T(1,128)S(1)}, u32[]{:S(2)}) copy-start(f32[1,512]{1,0:T(1,128)S(1)} %get-tuple-element.29) | copy-start | bytes 6148
  100.8 6.0 %copy-start.10 = (f32[1,512]{1,0:T(1,128)}, f32[1,512]{1,0:T(1,128)S(1)}, u32[]{:S(2)}) copy-start(f32[1,512]{1,0:T(1,128)S(1)} %get-tuple-element.30) | copy-start | bytes 6148
  100.8 6.0 %copy-start.11 = (f32[1,512]{1,0:T(1,128)}, f32[1,512]{1,0:T(1,128)S(1)}, u32[]{:S(2)}) copy-start(f32[1,512]{1,0:T(1,128)S(1)} %get-tuple-element.31) | copy-start | bytes 6148
  100.8 6.0 %copy-start.12 = (f32[1,512]{1,0:T(1,128)}, f32[1,512]{1,0:T(1,128)S(1)}, u32[]{:S(2)}) copy-start(f32[1,512]{1,0:T(1,128)S(1)} %get-tuple-element.32) | copy-start | bytes 6148
  106.8 1.3 copy-start
  108.1 131.2 %all-to-all-start = ((bf16[96,32,512]{2,0,1:T(8,128)(2,1)}), bf16[96,32,512]{2,0,1:T(8,128)(2,1)S(1)}, u32[]{:S(2)}, u32[]{:S(2)}) async-start(bf16[96,32,512]{2,0,1:T(8,128)(2,1)} %copy.24), calls=%async_computation | async-start | bytes 6291456 | tf_op jit(solution)/shard_map/all_to_all | solution.py:60
  114.4 113.6 %copy-start.4 = (f32[3,2048]{1,0:T(4,128)S(1)}, f32[3,2048]{1,0:T(4,128)}, u32[]{:S(2)}) copy-start(f32[3,2048]{1,0:T(4,128)} %param.17) | copy-start | bytes 73732
  114.4 113.6 %copy-start.2 = (s32[1,16384]{1,0:T(1,128)S(1)}, s32[1,16384]{1,0:T(1,128)}, u32[]{:S(2)}) copy-start(s32[1,16384]{1,0:T(1,128)} %param.13) | copy-start | bytes 196612
  344.8 17.4 %slice-start = ((s8[16777216]{0:T(1024)(128)(4,1)}), s8[4194304]{0:T(1024)(128)(4,1)S(1)}, s32[]{:S(2)}) async-start(s8[16777216]{0:T(1024)(128)(4,1)} %bitcast.55), calls=%async_computation.2 | async-start | bytes 8388608
  344.8 17.4 %slice-start.1 = ((s8[16777216]{0:T(1024)(128)(4,1)}), s8[4194304]{0:T(1024)(128)(4,1)S(1)}, s32[]{:S(2)}) async-start(s8[16777216]{0:T(1024)(128)(4,1)} %bitcast.55), calls=%async_computation.3 | async-start | bytes 8388608
  353.5 8.7 %slice-start.2 = ((s8[16777216]{0:T(1024)(128)(4,1)}), s8[4194304]{0:T(1024)(128)(4,1)S(1)}, s32[]{:S(2)}) async-start(s8[16777216]{0:T(1024)(128)(4,1)} %bitcast.55), calls=%async_computation.4 | async-start | bytes 8388608
  353.5 8.7 %slice-start.3 = ((s8[16777216]{0:T(1024)(128)(4,1)}), s8[4194304]{0:T(1024)(128)(4,1)S(1)}, s32[]{:S(2)}) async-start(s8[16777216]{0:T(1024)(128)(4,1)} %bitcast.55), calls=%async_computation.5 | async-start | bytes 8388608
where the time goes:
time: 367 us; the launch traced here: 366 us
  local copies, waits for them, and re-layouts  176 us (48%)
  other arithmetic  143 us (39%)
  matrix products  34.1 us (9%)
  starting transfers between devices  12.6 us (3%)
    convert_element_type x1, other arithmetic, blend_patch_major(): return blended.astype(jnp.bfloat16).reshape(rows, patches * support_count)  114 us
    gather x1, local copies, waits for them, and re-layouts, shards(): outgoing = jnp.take(displacement, send_index[0], axis=1)  57.7 us
    gather x1, local copies, waits for them, and re-layouts, shards(): jnp.take(arriving_rows, support[0], axis=1)  57.7 us
    dot_general x4, matrix products, shards(): jnp.einsum('cs,ns->cn', flat, blend, preferred_element_type=jnp.float32)  28.6 us
    unnamed x44, local copies, waits for them, and re-layouts  25.2 us
    select_n x1, other arithmetic, shards(): outgoing = jnp.take(displacement, send_index[0], axis=1)  11.5 us
    convert_element_type x1, local copies, waits for them, and re-layouts, shards(): coefficient = patch_products(own_inverse, values).astype(jnp.bfloat16)  11.2 us
    select_n x1, other arithmetic, shards(): jnp.take(arriving_rows, support[0], axis=1)  10.9 us
  transfers between devices with their start and end apart: 2, of which 0 were waited for; matrix products, arithmetic and copies ran while one was open for 58% of the time, Pallas kernels for 0%

commit v1 on v0

v1 whole, which is shorter than its diff:
```python
import functools

import jax
import jax.numpy as jnp
import numpy as np
from jax import lax
from jax.experimental import pallas as pl
from jax.experimental.pallas import tpu as pltpu
from jax.sharding import PartitionSpec as P

KERNEL_RADIUS = 0.45
ATTRACTION_REACH = 0.3
OWNER_PREMIUM = 8.0
LANES = 128
MIB = 1024 * 1024


def params(mib):
    return pltpu.CompilerParams(vmem_limit_bytes=mib * MIB)


def inverse_pack_kernel(inverse_ref, out_ref):
    half = inverse_ref.shape[0] // 2
    for a in range(half):
        pair = jnp.concatenate([inverse_ref[a], inverse_ref[a + half]], axis=0)
        turned = pair.astype(jnp.float32).T
        out_ref[0, :, a * LANES : (a + 1) * LANES] = turned.astype(jnp.bfloat16)


def inverse_pack(inverse, part, parts):
    rows, support_count, patches = inverse.shape
    windows = patches // (parts * LANES)
    return pl.pallas_call(
        inverse_pack_kernel,
        grid=(windows,),
        in_specs=[
            pl.BlockSpec((rows, support_count, LANES), lambda w: (0, 0, parts * w + part))
        ],
        out_specs=pl.BlockSpec((1, LANES, rows * support_count), lambda w: (w, 0, 0)),
        out_shape=jax.ShapeDtypeStruct((windows, LANES, rows * support_count), jnp.bfloat16),
        compiler_params=params(24),
        cost_estimate=pl.CostEstimate(
            flops=0, bytes_accessed=4 * inverse.size // parts, transcendentals=0
        ),
        name="inverse_pack",
    )(inverse)


def inverse_order(rows, support_count):
    half = rows // 2
    order = []
    for v in range(support_count // 16):
        for side in range(2):
            for i in range(8):
                r = 8 * v + i
                order.append((r // half) * rows + side * half + r % half)
    return np.array(order)


UNROLL = 32


def gather_rows(index_ref, source, target, base, count):
    def body(step, carry):
        for r in range(UNROLL):
            at = step * UNROLL + r
            target[pl.ds(at, 1), :] = source[pl.ds(index_ref[base + at], 1), :]
        return carry

    lax.fori_loop(0, count // UNROLL, body, 0)


def send_kernel(per, index_ref, displacement_ref, out_ref, rows_ref, block_ref):
    columns, nodes = displacement_ref.shape

    def turn(block, carry):
        at = pl.multiple_of(block * LANES, LANES)
        piece = displacement_ref[:, pl.ds(at, LANES)].astype(jnp.float32)
        piece = jnp.concatenate([piece, piece[: LANES - columns]], axis=0)
        rows_ref[pl.ds(at, LANES), :] = piece.T
        return carry

    lax.fori_loop(0, nodes // LANES, turn, 0)
    quarter = per // 4
    lane = lax.broadcasted_iota(jnp.int32, (quarter, LANES), 1)

    def peer(d, carry):
        gather_rows(index_ref, rows_ref, block_ref, d * per, per)
        last = block_ref[3 * quarter : 4 * quarter, :]
        for i in range(3):
            own = block_ref[i * quarter : (i + 1) * quarter, :]
            full = jnp.where(lane < 96, own, pltpu.roll(last, 96 - 32 * i, 1))
            at = pl.multiple_of(d * 3 * quarter + i * quarter, quarter)
            out_ref[pl.ds(at, quarter), :] = full.astype(jnp.bfloat16)
        return carry

    lax.fori_loop(0, nodes // per, peer, 0)


def send_rows(displacement, index, per):
    columns, nodes = displacement.shape
    return pl.pallas_call(
        functools.partial(send_kernel, per),
        in_specs=[
            pl.BlockSpec(memory_space=pltpu.SMEM),
            pl.BlockSpec(memory_space=pltpu.VMEM),
        ],
        out_specs=pl.BlockSpec(memory_space=pltpu.VMEM),
        out_shape=jax.ShapeDtypeStruct((nodes * 3 // 4, LANES), jnp.bfloat16),
        scratch_shapes=[
            pltpu.VMEM((nodes, LANES), jnp.float32),
            pltpu.VMEM((per, LANES), jnp.float32),
        ],
        compiler_params=params(32),
        cost_estimate=pl.CostEstimate(
            flops=0, bytes_accessed=60 * MIB, transcendentals=0
        ),
        name="send_rows",
    )(index, displacement)


def receive_kernel(per, index_ref, packed_ref, out_ref, rows_ref, block_ref):
    slots = rows_ref.shape[0]
    quarter = per // 4
    lane = lax.broadcasted_iota(jnp.int32, (quarter, LANES), 1)

    def peer(d, carry):
        parts = []
        for i in range(3):
            at = pl.multiple_of(d * 3 * quarter + i * quarter, quarter)
            piece = packed_ref[pl.ds(at, quarter), :].astype(jnp.float32)
            parts.append(pltpu.roll(piece, 32 * (i + 1), 1))
            to = pl.multiple_of(d * per + i * quarter, quarter)
            rows_ref[pl.ds(to, quarter), :] = piece
        last = jnp.where(lane < 32, parts[0], jnp.where(lane < 64, parts[1], parts[2]))
        to = pl.multiple_of(d * per + 3 * quarter, quarter)
        rows_ref[pl.ds(to, quarter), :] = last
        return carry

    lax.fori_loop(0, slots // per, peer, 0)
    chunk = block_ref.shape[0]

    def pick(b, carry):
        gather_rows(index_ref, rows_ref, block_ref, b * chunk, chunk)
        at = pl.multiple_of(b * chunk, chunk)
        out_ref[pl.ds(at, chunk), :] = block_ref[...].astype(jnp.bfloat16)
        return carry

    lax.fori_loop(0, slots // chunk, pick, 0)


def receive_rows(packed, index, per):
    slots = index.shape[0]
    return pl.pallas_call(
        functools.partial(receive_kernel, per),
        in_specs=[
            pl.BlockSpec(memory_space=pltpu.SMEM),
            pl.BlockSpec(memory_space=pltpu.VMEM),
        ],
        out_specs=pl.BlockSpec(memory_space=pltpu.VMEM),
        out_shape=jax.ShapeDtypeStruct((slots, LANES), jnp.bfloat16),
        scratch_shapes=[
            pltpu.VMEM((slots, LANES), jnp.float32),
            pltpu.VMEM((256, LANES), jnp.float32),
        ],
        compiler_params=params(32),
        cost_estimate=pl.CostEstimate(
            flops=0, bytes_accessed=60 * MIB, transcendentals=0
        ),
        name="receive_rows",
    )(index, packed)


def splits(x):
    high = x.astype(jnp.bfloat16).astype(jnp.float32)
    rest = x - high
    middle = rest.astype(jnp.bfloat16).astype(jnp.float32)
    return high, middle, rest - middle


def distance_rows(xyz, entry_side):
    rows = []
    square = None
    for c in range(3):
        x = xyz[c : c + 1, :] * (1.0 / KERNEL_RADIUS)
        square = x * x if square is None else square + x * x
        if entry_side:
            s1, s2, s3 = splits(-2.0 * x)
            rows += [s1, s1, s2, s2, s1, s3]
        else:
            p1, p2, p3 = splits(x)
            rows += [p1, p2, p1, p2, p3, p1]
    one = jnp.ones_like(square)
    own = list(splits(square))
    rows += own + [one] * 3 if entry_side else [one] * 3 + own
    rows += [jnp.zeros_like(square)] * 8
    return jnp.concatenate(rows, axis=0)


def falloff_terms(scaled_sq):
    safe = jnp.maximum(scaled_sq, 1e-12)
    return jnp.maximum(1.0 - safe * lax.rsqrt(safe), 0.0)


PANEL_CHUNK = 256


def blend_kernel(
    support_count,
    points_ref,
    member_ref,
    centers_ref,
    support_ref,
    out_ref,
    panel_rows,
    five_ref,
    four_ref,
):
    panels = points_ref.shape[1]
    patches = centers_ref.shape[0]
    entries = support_ref.shape[1]
    block_patches = entries // support_count
    step = pl.program_id(0)

    @pl.when(step == 0)
    def _():
        panel_rows[...] = distance_rows(points_ref[...], False).astype(jnp.bfloat16)
        patch = lax.broadcasted_iota(jnp.int32, (patches, LANES), 0)

        def weigh(b, carry):
            at = pl.multiple_of(b * LANES, LANES)
            square = None
            for c in range(3):
                gap = centers_ref[:, c : c + 1] - points_ref[c : c + 1, pl.ds(at, LANES)]
                square = gap * gap if square is None else square + gap * gap
            u = falloff_terms(square * (1.0 / ATTRACTION_REACH**2))
            u2 = u * u
            owner = jnp.where(member_ref[:, pl.ds(at, LANES)] == patch, OWNER_PREMIUM, 0.0)
            attraction = u2 * u2 * (5.0 - 4.0 * u) + owner
            weight = attraction / jnp.sum(attraction, axis=0, keepdims=True)
            five_ref[:, pl.ds(at, LANES)] = 5.0 * weight
            four_ref[:, pl.ds(at, LANES)] = 4.0 * weight
            return carry

        lax.fori_loop(0, panels // LANES, weigh, 0)

    entry_rows = distance_rows(support_ref[...], True).T.astype(jnp.bfloat16)

    def chunk(b, carry):
        at = pl.multiple_of(b * PANEL_CHUNK, PANEL_CHUNK)
        first = pl.multiple_of(step * block_patches, block_patches)
        five = five_ref[pl.ds(first, block_patches), pl.ds(at, PANEL_CHUNK)]
        four = four_ref[pl.ds(first, block_patches), pl.ds(at, PANEL_CHUNK)]
        columns = panel_rows[:, pl.ds(at, PANEL_CHUNK)]
        for p in range(block_patches):
            rows = slice(p * support_count, (p + 1) * support_count)
            square = jnp.dot(entry_rows[rows], columns, preferred_element_type=jnp.float32)
            u = falloff_terms(square)
            u2 = u * u
            value = u2 * u2 * (five[p : p + 1] - four[p : p + 1] * u)
            out_ref[rows, pl.ds(at, PANEL_CHUNK)] = value.astype(jnp.bfloat16)
        return carry

    lax.fori_loop(0, panels // PANEL_CHUNK, chunk, 0)


def blend_entry_major(points, member, support_xyz, centers, support_count):
    panels = points.shape[1]
    patches = centers.shape[1]
    slots = support_xyz.shape[1]
    block = 8 * support_count
    return pl.pallas_call(
        functools.partial(blend_kernel, support_count),
        grid=(slots // block,),
        in_specs=[
            pl.BlockSpec((3, panels), lambda i: (0, 0)),
            pl.BlockSpec((1, panels), lambda i: (0, 0)),
            pl.BlockSpec((patches, 3), lambda i: (0, 0)),
            pl.BlockSpec((3, block), lambda i: (0, i)),
        ],
        out_specs=pl.BlockSpec((block, panels), lambda i: (i, 0)),
        out_shape=jax.ShapeDtypeStruct((slots, panels), jnp.bfloat16),
        scratch_shapes=[
            pltpu.VMEM((32, panels), jnp.bfloat16),
            pltpu.VMEM((patches, panels), jnp.float32),
            pltpu.VMEM((patches, panels), jnp.float32),
        ],
        compiler_params=params(40),
        cost_estimate=pl.CostEstimate(
            flops=64 * slots * panels,
            bytes_accessed=4 * slots * panels,
            transcendentals=slots * panels,
        ),
        name="blend",
    )(points, member.reshape(1, panels), centers.T, support_xyz)


def moved_kernel(modes, last, support_count, *refs):
    if last:
        inverse_ref, values_ref, blend_ref, start_ref, normals_ref, out_ref = refs[:6]
        turned_ref, total_ref, coef_ref = refs[6:]
    else:
        inverse_ref, values_ref, blend_ref, out_ref = refs[:4]
        turned_ref, coef_ref = refs[4:]
        total_ref = out_ref
    step = pl.program_id(0)

    @pl.when(step == 0)
    def _():
        if last:
            total_ref[...] = start_ref[...]
        else:
            total_ref[...] = jnp.zeros_like(total_ref)

    owners, block_patches, width = inverse_ref.shape
    halves = width // LANES
    per_patch = owners * halves
    for o in range(owners):
        for a in range(halves):
            piece = inverse_ref[o, :, a * LANES : (a + 1) * LANES].astype(jnp.float32)
            turned_ref[pl.ds(o * halves + a, block_patches, stride=per_patch), :] = piece
    lane = lax.broadcasted_iota(jnp.int32, (8, LANES), 1)
    low = lane < support_count
    for pair in range(block_patches // 2):
        rows = []
        for side in range(2):
            for v in range(per_patch // 8):
                at = (2 * pair + side) * per_patch + 8 * v
                own = turned_ref[at : at + 8, :]
                other = pltpu.roll(own, support_count, 1)
                both = (own, other) if side == 0 else (other, own)
                keep = low if side == 0 else jnp.logical_not(low)
                rows += [jnp.where(keep, x, 0.0) for x in both]
        block = jnp.concatenate(rows, axis=0).astype(jnp.bfloat16)
        at = pair * LANES
        coef = jnp.dot(
            block, values_ref[at : at + LANES, :], preferred_element_type=jnp.float32
        )
        coef_ref[:, at : at + LANES] = coef.T[: 3 * modes].astype(jnp.bfloat16)
    total_ref[...] += jnp.dot(
        coef_ref[...], blend_ref[...], preferred_element_type=jnp.float32
    )

    if last:

        @pl.when(step == pl.num_programs(0) - 1)
        def _():
            result = None
            for c in range(3):
                term = normals_ref[c : c + 1, :] * total_ref[c * modes : (c + 1) * modes, :]
                result = term if result is None else result + term
            out_ref[...] = result


def moved_part(inverse, values, blend, part, modes, support_count, start=None, normals=None):
    owners, patches, width = inverse.shape
    slots, panels = blend.shape
    block_patches = 16
    steps = patches // block_patches
    block = block_patches * support_count
    last = start is not None
    in_specs = [
        pl.BlockSpec((owners, block_patches, width), lambda i: (0, i, 0)),
        pl.BlockSpec((block, LANES), lambda i: (part * steps + i, 0)),
        pl.BlockSpec((block, panels), lambda i: (part * steps + i, 0)),
    ]
    operands = [inverse, values, blend]
    total_shape = (3 * modes, panels)
    scratch = [pltpu.VMEM((block_patches * support_count // 2, LANES), jnp.float32)]
    if last:
        in_specs += [
            pl.BlockSpec(total_shape, lambda i: (0, 0)),
            pl.BlockSpec((3, panels), lambda i: (0, 0)),
        ]
        operands += [start, normals]
        scratch += [pltpu.VMEM(total_shape, jnp.float32)]
        out_shape = (modes, panels)
    else:
        out_shape = total_shape
    scratch += [pltpu.VMEM((3 * modes, block), jnp.bfloat16)]
    return pl.pallas_call(
        functools.partial(moved_kernel, modes, last, support_count),
        grid=(steps,),
        in_specs=in_specs,
        out_specs=pl.BlockSpec(out_shape, lambda i: (0, 0)),
        out_shape=jax.ShapeDtypeStruct(out_shape, jnp.float32),
        scratch_shapes=scratch,
        compiler_params=params(40),
        cost_estimate=pl.CostEstimate(
            flops=2 * 3 * modes * panels * patches * support_count,
            bytes_accessed=2 * panels * patches * support_count,
            transcendentals=0,
        ),
        name="moved_last" if last else "moved_first",
    )(*operands)


def shards(

    displacement,
    send_index,
    support,
    support_xyz,
    patch_kernel_inverse,
    panel_xyz,
    normals,
    centers,
    member,
):
    axes = ("panel", "group")
    columns = displacement.shape[0]
    modes = columns // 3
    slots = send_index.shape[1]
    patches = centers.shape[1]
    support_count = slots // patches
    devices = lax.axis_size(axes)
    per = slots // devices
    parts = patches // LANES

    own_rows = patch_kernel_inverse.shape[0]
    order = inverse_order(own_rows, support_count)
    if not np.array_equal(order, np.arange(support_count)):
        xyz = support_xyz.reshape(3, patches, support_count)
        support_xyz = jnp.take(xyz, order, axis=2).reshape(3, slots)

    def exchange(packed):
        got = lax.all_to_all(packed, "group", split_axis=0, concat_axis=0, tiled=True)
        return got

    first = exchange(inverse_pack(patch_kernel_inverse, 0, parts))
    second_packed = inverse_pack(patch_kernel_inverse, 1, parts)
    outgoing = send_rows(displacement, send_index.reshape(slots), per)
    arriving = lax.all_to_all(
        outgoing.reshape(devices, per * 3 // 4, LANES), axes, 0, 0, tiled=True
    ).reshape(slots * 3 // 4, LANES)
    second_packed, _ = lax.optimization_barrier((second_packed, outgoing))
    second = exchange(second_packed)
    blend = blend_entry_major(panel_xyz, member, support_xyz, centers, support_count)
    values = receive_rows(arriving, support.reshape(slots), per)
    total = moved_part(first, values, blend, 0, modes, support_count)
    return moved_part(second, values, blend, 1, modes, support_count, total, normals)


def solution(mesh):
    return jax.shard_map(
        shards,
        mesh=mesh,
        in_specs=(
            P(None, ("panel", "group")),
            P(("panel", "group"), None),
            P(("panel", "group"), None),
            P(None, ("panel", "group")),
            P("group", None, "panel"),
            P(None, ("panel", "group")),
            P(None, ("panel", "group")),
            P(None, ("panel", "group")),
            P(("panel", "group")),
        ),
        out_specs=P(None, ("panel", "group")),
        check_vma=False,
    )
```

time: 367 us -> 294 us (0.80)
  Pallas kernels: 0 us -> 195 us
  local copies, waits for them, and re-layouts: 176 us -> 13.7 us
  other arithmetic: 143 us -> 0 us
  waiting for transfers between devices: 0.01 us -> 66.7 us
  matrix products: 34.1 us -> 0 us
  starting transfers between devices: 12.6 us -> 16.7 us
    pallas_call x0 -> x7, Pallas kernels: none -> 195 us  [the longest x1 98.5 us: blend_entry_major(): pl.pallas_call(functools.partial(blend_kernel, support_count), grid=(slot...]
    gather x2 -> x0, local copies, waits for them, and re-layouts: 115 us -> none  [the longest x1 57.7 us: shards(): outgoing = jnp.take(displacement, send_index[0], axis=1)]
    convert_element_type x1 -> x0, other arithmetic: 114 us -> none  [blend_patch_major(): return blended.astype(jnp.bfloat16).reshape(rows, patches * support_count)]
    all_to_all x2 -> x3, waiting for transfers between devices: 0.01 us -> 66.7 us  [the longest x1 66.7 us: shards(): lax.all_to_all(outgoing.reshape(devices, per * 3 // 4, LANES), axes, 0, 0...]
    dot_general x5 -> x0, matrix products: 34.1 us -> none  [the longest x4 28.6 us: shards(): jnp.einsum('cs,ns->cn', flat, blend, preferred_element_type=jnp.float32)]
    select_n x2 -> x0, other arithmetic: 22.5 us -> none  [the longest x1 11.5 us: shards(): outgoing = jnp.take(displacement, send_index[0], axis=1)]
    all_to_all x3 -> x0, local copies, waits for them, and re-layouts: 16 us -> none  [the longest x2 10.5 us: shards(): lax.all_to_all(outgoing, ('panel', 'group'), split_axis=1, concat_axis=1,...]
    unnamed x44 -> x33, local copies, waits for them, and re-layouts: 25.2 us -> 13.7 us
  transfers between devices with their start and end apart: 2 -> 3, of which waited for: 0 -> 1; matrix products, arithmetic and copies ran while one was open for 58% -> 0% of each run, Pallas kernels for 0% -> 60%
where the time goes in v1:
time: 294 us; the launch traced here: 292 us
  Pallas kernels  195 us (66%)
  waiting for transfers between devices  66.7 us (23%)
  starting transfers between devices  16.7 us (6%)
  local copies, waits for them, and re-layouts  13.7 us (5%)
    pallas_call x1, Pallas kernels, blend_entry_major(): pl.pallas_call(functools.partial(blend_kernel, support_count), grid=(slot...  98.5 us
    all_to_all x1, waiting for transfers between devices, shards(): lax.all_to_all(outgoing.reshape(devices, per * 3 // 4, LANES), axes, 0, 0...  66.7 us
    pallas_call x1, Pallas kernels, send_rows(): pl.pallas_call(functools.partial(send_kernel, per), in_specs=[pl.BlockSpe...  37 us
    pallas_call x2, Pallas kernels, moved_part(): pl.pallas_call(functools.partial(moved_kernel, modes, last, support_count...  31.9 us
    pallas_call x1, Pallas kernels, receive_rows(): pl.pallas_call(functools.partial(receive_kernel, per), in_specs=[pl.Block...  24.7 us
    unnamed x33, local copies, waits for them, and re-layouts  13.7 us
    all_to_all x2, starting transfers between devices, exchange(): lax.all_to_all(packed, 'group', split_axis=0, concat_axis=0, tiled=True)  10.7 us
    all_to_all x1, starting transfers between devices, shards(): lax.all_to_all(outgoing.reshape(devices, per * 3 // 4, LANES), axes, 0, 0...  6.07 us
  transfers between devices with their start and end apart: 3, of which 1 were waited for; matrix products, arithmetic and copies ran while one was open for 0% of the time, Pallas kernels for 60%

profile of v1, /device:TPU:0, one launch (start us, length us, event | category | flops | bytes accessed | tf_op | source)
XLA Modules:
  0.0 292.3 jit_solution(17740487459015928736)
XLA Ops:
  0.0 0.0 copy-start.3
  0.0 1.6 copy-done.3
  1.6 0.0 copy-start.10
  1.6 2.0 inverse_pack.3
  3.6 6.3 %all-to-all-start.2 = ((bf16[4,128,1024]{2,1,0:T(8,128)(2,1)}), bf16[4,128,1024]{2,1,0:T(8,128)(2,1)S(1)}, u32[]{:S(2)}, u32[]{:S(2)}) async-start(bf16[4,128,1024]{2,1,0:T(8,128)(2,1)} %inverse_pack.3), calls=%async_computation.2 | async-start | bytes 2097152 | tf_op jit(solution)/shard_map/all_to_all | solution.py:427
  10.0 0.0 copy-done.10
  10.0 0.0 copy-start.8
  10.0 1.9 copy-done.8
  11.8 37.0 %send_rows.1 = bf16[12288,128]{1,0:T(8,128)(2,1)S(1)} custom-call(s32[16384]{0:T(1024)S(1)} %bitcast.9, bf16[96,16384]{1,0:T(8,128)(2,1)S(1)} %copy-done.8), custom_call_target="tpu_custom_call" | custom-call | bytes 62914560 | tf_op jit(solution)/shard_map/send_rows/pallas_call | solution.py:102
  48.8 0.0 copy-start.2
  48.9 1.6 copy-done.2
  50.5 0.0 all-to-all-done.2.refs_0_
  50.5 0.0 copy-start.5
  50.5 1.0 copy-done.5
  51.5 6.1 %all-to-all-start.1 = ((bf16[32,384,128]{2,1,0:T(8,128)(2,1)}), bf16[32,384,128]{2,1,0:T(8,128)(2,1)S(1)}, u32[]{:S(2)}, u32[]{:S(2)}) async-start(bf16[32,384,128]{2,1,0:T(8,128)(2,1)} %bitcast.7), calls=%async_computation.1 | async-start | bytes 6291456 | tf_op jit(solution)/shard_map/all_to_all | solution.py:433
  57.6 0.0 copy-start.4
  57.6 1.6 copy-done.4
  59.1 0.0 copy-start.15
  59.2 0.0 copy-start.9
  59.2 0.0 copy-start.14
  59.2 0.9 inverse_pack.2
  60.1 0.0 copy-start.7
  60.1 1.0 copy-done.7
  61.0 66.7 %all-to-all-done.1 = bf16[32,384,128]{2,1,0:T(8,128)(2,1)S(1)} async-done(((bf16[32,384,128]{2,1,0:T(8,128)(2,1)}), bf16[32,384,128]{2,1,0:T(8,128)(2,1)S(1)}, u32[]{:S(2)}, u32[]{:S(2)}) %all-to-all-start.1) | async-done | bytes 3145760 | tf_op jit(solution)/shard_map/all_to_all | solution.py:433
  127.7 4.3 %all-to-all-start = ((bf16[4,128,1024]{2,1,0:T(8,128)(2,1)}), bf16[4,128,1024]{2,1,0:T(8,128)(2,1)}, u32[]{:S(2)}, u32[]{:S(2)}) async-start(bf16[4,128,1024]{2,1,0:T(8,128)(2,1)} %copy-done.7), calls=%async_computation | async-start | bytes 2097152 | tf_op jit(solution)/shard_map/all_to_all | solution.py:427
  132.1 0.0 copy-done.15
  132.1 0.1 copy.10
  132.2 0.0 copy-done.9
  132.2 0.0 copy-done.14
  132.2 0.0 copy-start.12
  132.2 0.7 copy-done.12
  133.0 0.0 copy-start.11
  133.0 98.5 %blend.1.refs_2_ = bf16[16384,2048]{1,0:T(8,128)(2,1)} custom-call(f32[3,2048]{1,0:T(4,128)S(1)} %copy-done.12, s32[1,2048]{1,0:T(1,128)S(1)} %bitcast.11, f32[256,3]{1,0:T(8,128)S(1)} %bitcast.8, f32[3,16384]{1,0:T(4,128)S(1)} %copy-done.9), custom_call_target="tpu_custom_call" | custom-call | flops 2147483648 | bytes 134217728 | tf_op jit(solution)/shard_map/blend/pallas_call | solution.py:272
  231.5 0.0 copy-done.11
  231.5 0.0 copy-start.6
  231.5 24.7 %receive_rows.1.refs_1_ = bf16[16384,128]{1,0:T(8,128)(2,1)S(1)} custom-call(s32[16384]{0:T(1024)S(1)} %bitcast.10, bf16[12288,128]{1,0:T(8,128)(2,1)S(1)} %bitcast.6), custom_call_target="tpu_custom_call" | custom-call | bytes 62914560 | tf_op jit(solution)/shard_map/receive_rows/pallas_call | solution.py:154
  256.2 0.0 copy-done.6
  256.2 0.0 copy-start.13
  256.2 15.4 %moved_first.1.refs_3_ = f32[96,2048]{1,0:T(8,128)S(1)} custom-call(bf16[4,128,1024]{2,1,0:T(8,128)(2,1)S(1)} %copy-done.6, bf16[16384,128]{1,0:T(8,128)(2,1)S(1)} %receive_rows.1.refs_1_, bf16[16384,2048]{1,0:T(8,128)(2,1)} %blend.1.refs_2_), custom_call_target="tpu_custom_call" | custom-call | flops 3221225472 | bytes 33554432 | tf_op jit(solution)/shard_map/moved_first/pallas_call | solution.py:381
  271.7 0.0 copy-start
  271.7 2.0 copy-done
  273.7 0.0 all-to-all-done.refs_0_
  273.7 0.0 copy-done.13
  273.7 0.0 copy-start.1
  273.7 2.2 copy-done.1
  275.9 16.4 %moved_last.1 = f32[32,2048]{1,0:T(8,128)} custom-call(bf16[4,128,1024]{2,1,0:T(8,128)(2,1)} %all-to-all-done.refs_0_, bf16[16384,128]{1,0:T(8,128)(2,1)S(1)} %copy-done.1, bf16[16384,2048]{1,0:T(8,128)(2,1)} %blend.1.refs_2_, f32[96,2048]{1,0:T(8,128)S(1)} %moved_first.1.refs_3_, f32[3,2048]{1,0:T(4,128)S(1)} %copy-done.13), custom_call_target="tpu_custom_call" | custom-call | flops 3221225472 | bytes 33554432 | tf_op jit(solution)/shard_map/moved_last/pallas_call | solution.py:381
Async XLA Ops:
  0.0 1.6 copy-start.3
  1.6 8.4 %copy-start.10 = (s32[1,16384]{1,0:T(1,128)S(1)}, s32[1,16384]{1,0:T(1,128)}, u32[]{:S(2)}) copy-start(s32[1,16384]{1,0:T(1,128)} %param.10) | copy-start | bytes 196612
  3.6 46.9 %all-to-all-start.2 = ((bf16[4,128,1024]{2,1,0:T(8,128)(2,1)}), bf16[4,128,1024]{2,1,0:T(8,128)(2,1)S(1)}, u32[]{:S(2)}, u32[]{:S(2)}) async-start(bf16[4,128,1024]{2,1,0:T(8,128)(2,1)} %inverse_pack.3), calls=%async_computation.2 | async-start | bytes 2097152 | tf_op jit(solution)/shard_map/all_to_all | solution.py:427
  10.0 1.9 copy-start.8
  48.8 1.7 copy-start.2
  50.5 1.0 copy-start.5
  51.5 76.2 %all-to-all-start.1 = ((bf16[32,384,128]{2,1,0:T(8,128)(2,1)}), bf16[32,384,128]{2,1,0:T(8,128)(2,1)S(1)}, u32[]{:S(2)}, u32[]{:S(2)}) async-start(bf16[32,384,128]{2,1,0:T(8,128)(2,1)} %bitcast.7), calls=%async_computation.1 | async-start | bytes 6291456 | tf_op jit(solution)/shard_map/all_to_all | solution.py:433
  57.6 1.6 copy-start.4
  59.1 72.9 %copy-start.15 = (f32[3,256]{1,0:T(4,128)S(1)}, f32[3,256]{1,0:T(4,128)}, u32[]{:S(2)}) copy-start(f32[3,256]{1,0:T(4,128)} %param.16) | copy-start | bytes 9220
  59.2 73.0 %copy-start.9 = (f32[3,16384]{1,0:T(4,128)S(1)}, f32[3,16384]{1,0:T(4,128)}, u32[]{:S(2)}) copy-start(f32[3,16384]{1,0:T(4,128)} %support_ref.1) | copy-start | bytes 589828
  59.2 73.1 %copy-start.14 = (s32[2048]{0:T(1024)S(1)}, s32[2048]{0:T(1024)}, u32[]{:S(2)}) copy-start(s32[2048]{0:T(1024)} %param.17) | copy-start | bytes 24580
  60.1 1.0 copy-start.7
  127.7 146.0 %all-to-all-start = ((bf16[4,128,1024]{2,1,0:T(8,128)(2,1)}), bf16[4,128,1024]{2,1,0:T(8,128)(2,1)}, u32[]{:S(2)}, u32[]{:S(2)}) async-start(bf16[4,128,1024]{2,1,0:T(8,128)(2,1)} %copy-done.7), calls=%async_computation | async-start | bytes 2097152 | tf_op jit(solution)/shard_map/all_to_all | solution.py:427
  132.2 0.8 copy-start.12
  133.0 98.5 %copy-start.11 = (s32[1,16384]{1,0:T(1,128)S(1)}, s32[1,16384]{1,0:T(1,128)}, u32[]{:S(2)}) copy-start(s32[1,16384]{1,0:T(1,128)} %param.11) | copy-start | bytes 196612
  231.5 24.7 %copy-start.6 = (bf16[4,128,1024]{2,1,0:T(8,128)(2,1)S(1)}, bf16[4,128,1024]{2,1,0:T(8,128)(2,1)}, u32[]{:S(2)}) copy-start(bf16[4,128,1024]{2,1,0:T(8,128)(2,1)} %copy-done.5) | copy-start | bytes 3145732
  256.2 17.5 %copy-start.13 = (f32[3,2048]{1,0:T(4,128)S(1)}, f32[3,2048]{1,0:T(4,128)}, u32[]{:S(2)}) copy-start(f32[3,2048]{1,0:T(4,128)} %refs_4_.1) | copy-start | bytes 73732
  271.7 2.0 copy-start
  273.7 2.2 copy-start.1

commit v2 on v1

--- a/solution.py
+++ b/solution.py
@@ -430,12 +430,13 @@
     first = exchange(inverse_pack(patch_kernel_inverse, 0, parts))
     second_packed = inverse_pack(patch_kernel_inverse, 1, parts)
     outgoing = send_rows(displacement, send_index.reshape(slots), per)
+    outgoing, panel_xyz = lax.optimization_barrier((outgoing, panel_xyz))
     arriving = lax.all_to_all(
         outgoing.reshape(devices, per * 3 // 4, LANES), axes, 0, 0, tiled=True
     ).reshape(slots * 3 // 4, LANES)
-    second_packed, _ = lax.optimization_barrier((second_packed, outgoing))
+    blend = blend_entry_major(panel_xyz, member, support_xyz, centers, support_count)
+    blend, second_packed, support = lax.optimization_barrier((blend, second_packed, support))
     second = exchange(second_packed)
-    blend = blend_entry_major(panel_xyz, member, support_xyz, centers, support_count)
     values = receive_rows(arriving, support.reshape(slots), per)
     total = moved_part(first, values, blend, 0, modes, support_count)
     return moved_part(second, values, blend, 1, modes, support_count, total, normals)

time: 294 us -> 228 us (0.78)
  waiting for transfers between devices: 66.7 us -> 0.01 us
    all_to_all x1, waiting for transfers between devices: 66.7 us -> 0.01 us  [shards(): lax.all_to_all(outgoing.reshape(devices, per * 3 // 4, LANES), axes, 0, 0...]
  transfers between devices with their start and end apart: 3 -> 3, of which waited for: 1 -> 0; matrix products, arithmetic and copies ran while one was open for 0% -> 0% of each run, Pallas kernels for 60% -> 78%
where the time goes in v2:
time: 228 us; the launch traced here: 227 us
  Pallas kernels  195 us (86%)
  starting transfers between devices  17.3 us (8%)
  local copies, waits for them, and re-layouts  14.6 us (6%)
    pallas_call x1, Pallas kernels, blend_entry_major(): pl.pallas_call(functools.partial(blend_kernel, support_count), grid=(slot...  98.8 us
    pallas_call x1, Pallas kernels, send_rows(): pl.pallas_call(functools.partial(send_kernel, per), in_specs=[pl.BlockSpe...  37 us
    pallas_call x2, Pallas kernels, moved_part(): pl.pallas_call(functools.partial(moved_kernel, modes, last, support_count...  31.9 us
    pallas_call x1, Pallas kernels, receive_rows(): pl.pallas_call(functools.partial(receive_kernel, per), in_specs=[pl.Block...  24.7 us
    unnamed x33, local copies, waits for them, and re-layouts  14.6 us
    all_to_all x2, starting transfers between devices, exchange(): lax.all_to_all(packed, 'group', split_axis=0, concat_axis=0, tiled=True)  11.2 us
    all_to_all x1, starting transfers between devices, shards(): lax.all_to_all(outgoing.reshape(devices, per * 3 // 4, LANES), axes, 0, 0...  6.07 us
  transfers between devices with their start and end apart: 3, of which 0 were waited for; matrix products, arithmetic and copies ran while one was open for 0% of the time, Pallas kernels for 78%

profile of v2, /device:TPU:0, one launch (start us, length us, event | category | flops | bytes accessed | tf_op | source)
XLA Modules:
  0.0 227.3 jit_solution(13065912446919326911)
XLA Ops:
  0.0 0.0 copy-start.3
  0.0 1.6 copy-done.3
  1.6 0.0 copy-start.10
  1.6 2.0 inverse_pack.3
  3.6 6.3 %all-to-all-start.2 = ((bf16[4,128,1024]{2,1,0:T(8,128)(2,1)}), bf16[4,128,1024]{2,1,0:T(8,128)(2,1)S(1)}, u32[]{:S(2)}, u32[]{:S(2)}) async-start(bf16[4,128,1024]{2,1,0:T(8,128)(2,1)} %inverse_pack.3), calls=%async_computation.2 | async-start | bytes 2097152 | tf_op jit(solution)/shard_map/all_to_all | solution.py:427
  10.0 0.0 copy-done.10
  10.0 0.0 copy-start.8
  10.0 1.9 copy-done.8
  11.9 37.0 %send_rows.1 = bf16[12288,128]{1,0:T(8,128)(2,1)S(1)} custom-call(s32[16384]{0:T(1024)S(1)} %bitcast.9, bf16[96,16384]{1,0:T(8,128)(2,1)S(1)} %copy-done.8), custom_call_target="tpu_custom_call" | custom-call | bytes 62914560 | tf_op jit(solution)/shard_map/send_rows/pallas_call | solution.py:102
  48.8 0.0 copy-start.2
  48.9 1.7 copy-done.2
  50.5 0.0 all-to-all-done.2.refs_0_
  50.5 0.0 copy-start.5
  50.5 1.0 copy-done.5
  51.5 6.1 %all-to-all-start.1 = ((bf16[32,384,128]{2,1,0:T(8,128)(2,1)}), bf16[32,384,128]{2,1,0:T(8,128)(2,1)S(1)}, u32[]{:S(2)}, u32[]{:S(2)}) async-start(bf16[32,384,128]{2,1,0:T(8,128)(2,1)} %bitcast.7), calls=%async_computation.1 | async-start | bytes 6291456 | tf_op jit(solution)/shard_map/all_to_all | solution.py:434
  57.6 0.0 copy-start.4
  57.6 1.6 copy-done.4
  59.2 0.0 copy-start.15
  59.2 0.0 copy-start.9
  59.2 0.0 copy-start.14
  59.2 0.9 inverse_pack.2
  60.1 0.0 copy-start.7
  60.1 1.0 copy-done.7
  61.1 0.0 copy-done.15
  61.1 0.1 copy.10
  61.2 0.0 copy-done.9
  61.2 0.0 copy-done.14
  61.2 0.0 copy-start.12
  61.3 0.7 copy-done.12
  62.0 98.8 %blend.1.refs_2_ = bf16[16384,2048]{1,0:T(8,128)(2,1)} custom-call(f32[3,2048]{1,0:T(4,128)S(1)} %copy-done.12, s32[1,2048]{1,0:T(1,128)S(1)} %bitcast.11, f32[256,3]{1,0:T(8,128)S(1)} %bitcast.8, f32[3,16384]{1,0:T(4,128)S(1)} %copy-done.9), custom_call_target="tpu_custom_call" | custom-call | flops 2147483648 | bytes 134217728 | tf_op jit(solution)/shard_map/blend/pallas_call | solution.py:272
  160.8 0.0 all-to-all-done.1
  160.8 4.9 %all-to-all-start = ((bf16[4,128,1024]{2,1,0:T(8,128)(2,1)}), bf16[4,128,1024]{2,1,0:T(8,128)(2,1)}, u32[]{:S(2)}, u32[]{:S(2)}) async-start(bf16[4,128,1024]{2,1,0:T(8,128)(2,1)} %copy-done.7), calls=%async_computation | async-start | bytes 2097152 | tf_op jit(solution)/shard_map/all_to_all | solution.py:427
  165.7 0.0 copy-start.11
  165.7 0.8 copy-done.11
  166.5 0.0 copy-start.6
  166.5 24.7 %receive_rows.1.refs_1_ = bf16[16384,128]{1,0:T(8,128)(2,1)S(1)} custom-call(s32[16384]{0:T(1024)S(1)} %bitcast.10, bf16[12288,128]{1,0:T(8,128)(2,1)S(1)} %bitcast.6), custom_call_target="tpu_custom_call" | custom-call | bytes 62914560 | tf_op jit(solution)/shard_map/receive_rows/pallas_call | solution.py:154
  191.2 0.0 copy-done.6
  191.2 0.0 copy-start.13
  191.2 15.4 %moved_first.1.refs_3_ = f32[96,2048]{1,0:T(8,128)S(1)} custom-call(bf16[4,128,1024]{2,1,0:T(8,128)(2,1)S(1)} %copy-done.6, bf16[16384,128]{1,0:T(8,128)(2,1)S(1)} %receive_rows.1.refs_1_, bf16[16384,2048]{1,0:T(8,128)(2,1)} %blend.1.refs_2_), custom_call_target="tpu_custom_call" | custom-call | flops 3221225472 | bytes 33554432 | tf_op jit(solution)/shard_map/moved_first/pallas_call | solution.py:381
  206.7 0.0 copy-start
  206.7 2.0 copy-done
  208.7 0.0 all-to-all-done.refs_0_
  208.7 0.0 copy-done.13
  208.7 0.0 copy-start.1
  208.7 2.2 copy-done.1
  210.9 16.4 %moved_last.1 = f32[32,2048]{1,0:T(8,128)} custom-call(bf16[4,128,1024]{2,1,0:T(8,128)(2,1)} %all-to-all-done.refs_0_, bf16[16384,128]{1,0:T(8,128)(2,1)S(1)} %copy-done.1, bf16[16384,2048]{1,0:T(8,128)(2,1)} %blend.1.refs_2_, f32[96,2048]{1,0:T(8,128)S(1)} %moved_first.1.refs_3_, f32[3,2048]{1,0:T(4,128)S(1)} %copy-done.13), custom_call_target="tpu_custom_call" | custom-call | flops 3221225472 | bytes 33554432 | tf_op jit(solution)/shard_map/moved_last/pallas_call | solution.py:381
Async XLA Ops:
  0.0 1.6 copy-start.3
  1.6 8.4 %copy-start.10 = (s32[1,16384]{1,0:T(1,128)S(1)}, s32[1,16384]{1,0:T(1,128)}, u32[]{:S(2)}) copy-start(s32[1,16384]{1,0:T(1,128)} %param.10) | copy-start | bytes 196612
  3.6 46.9 %all-to-all-start.2 = ((bf16[4,128,1024]{2,1,0:T(8,128)(2,1)}), bf16[4,128,1024]{2,1,0:T(8,128)(2,1)S(1)}, u32[]{:S(2)}, u32[]{:S(2)}) async-start(bf16[4,128,1024]{2,1,0:T(8,128)(2,1)} %inverse_pack.3), calls=%async_computation.2 | async-start | bytes 2097152 | tf_op jit(solution)/shard_map/all_to_all | solution.py:427
  10.0 1.9 copy-start.8
  48.8 1.7 copy-start.2
  50.5 1.0 copy-start.5
  51.5 109.3 %all-to-all-start.1 = ((bf16[32,384,128]{2,1,0:T(8,128)(2,1)}), bf16[32,384,128]{2,1,0:T(8,128)(2,1)S(1)}, u32[]{:S(2)}, u32[]{:S(2)}) async-start(bf16[32,384,128]{2,1,0:T(8,128)(2,1)} %bitcast.7), calls=%async_computation.1 | async-start | bytes 6291456 | tf_op jit(solution)/shard_map/all_to_all | solution.py:434
  57.6 1.6 copy-start.4
  59.2 1.9 copy-start.15
  59.2 2.0 copy-start.9
  59.2 2.0 copy-start.14
  60.1 1.0 copy-start.7
  61.2 0.8 copy-start.12
  160.8 47.9 %all-to-all-start = ((bf16[4,128,1024]{2,1,0:T(8,128)(2,1)}), bf16[4,128,1024]{2,1,0:T(8,128)(2,1)}, u32[]{:S(2)}, u32[]{:S(2)}) async-start(bf16[4,128,1024]{2,1,0:T(8,128)(2,1)} %copy-done.7), calls=%async_computation | async-start | bytes 2097152 | tf_op jit(solution)/shard_map/all_to_all | solution.py:427
  165.7 0.8 copy-start.11
  166.5 24.7 %copy-start.6 = (bf16[4,128,1024]{2,1,0:T(8,128)(2,1)S(1)}, bf16[4,128,1024]{2,1,0:T(8,128)(2,1)}, u32[]{:S(2)}) copy-start(bf16[4,128,1024]{2,1,0:T(8,128)(2,1)} %copy-done.5) | copy-start | bytes 3145732
  191.2 17.5 %copy-start.13 = (f32[3,2048]{1,0:T(4,128)S(1)}, f32[3,2048]{1,0:T(4,128)}, u32[]{:S(2)}) copy-start(f32[3,2048]{1,0:T(4,128)} %refs_4_.1) | copy-start | bytes 73732
  206.7 2.0 copy-start
  208.7 2.2 copy-start.1

commit v3 on v1

--- a/solution.py
+++ b/solution.py
@@ -19,31 +19,37 @@
     return pltpu.CompilerParams(vmem_limit_bytes=mib * MIB)
 
 
-def inverse_pack_kernel(inverse_ref, out_ref):
+def inverse_pack_kernel(window_ref, inverse_ref, out_ref):
     half = inverse_ref.shape[0] // 2
     for a in range(half):
         pair = jnp.concatenate([inverse_ref[a], inverse_ref[a + half]], axis=0)
         turned = pair.astype(jnp.float32).T
-        out_ref[0, :, a * LANES : (a + 1) * LANES] = turned.astype(jnp.bfloat16)
-
-
-def inverse_pack(inverse, part, parts):
-    rows, support_count, patches = inverse.shape
-    windows = patches // (parts * LANES)
+        out_ref[:, a * LANES : (a + 1) * LANES] = turned.astype(jnp.bfloat16)
+
+
+def inverse_pack(inverse, window, patches):
+    rows, support_count, _ = inverse.shape
+    parts = patches // LANES
+    width = rows * support_count
     return pl.pallas_call(
         inverse_pack_kernel,
-        grid=(windows,),
-        in_specs=[
-            pl.BlockSpec((rows, support_count, LANES), lambda w: (0, 0, parts * w + part))
-        ],
-        out_specs=pl.BlockSpec((1, LANES, rows * support_count), lambda w: (w, 0, 0)),
-        out_shape=jax.ShapeDtypeStruct((windows, LANES, rows * support_count), jnp.bfloat16),
+        grid_spec=pltpu.PrefetchScalarGridSpec(
+            num_scalar_prefetch=1,
+            grid=(parts,),
+            in_specs=[
+                pl.BlockSpec(
+                    (rows, support_count, LANES), lambda i, w: (0, 0, parts * w[0] + i)
+                )
+            ],
+            out_specs=pl.BlockSpec((LANES, width), lambda i, w: (i, 0)),
+        ),
+        out_shape=jax.ShapeDtypeStruct((patches, width), jnp.bfloat16),
         compiler_params=params(24),
         cost_estimate=pl.CostEstimate(
-            flops=0, bytes_accessed=4 * inverse.size // parts, transcendentals=0
+            flops=0, bytes_accessed=4 * patches * width, transcendentals=0
         ),
         name="inverse_pack",
-    )(inverse)
+    )(window.reshape(1), inverse)
 
 
 def inverse_order(rows, support_count):
@@ -57,7 +63,7 @@
     return np.array(order)
 
 
-UNROLL = 32
+UNROLL = 128
 
 
 def gather_rows(index_ref, source, target, base, count):
@@ -80,7 +86,7 @@
         rows_ref[pl.ds(at, LANES), :] = piece.T
         return carry
 
-    lax.fori_loop(0, nodes // LANES, turn, 0)
+    lax.fori_loop(0, nodes // LANES, turn, 0, unroll=4)
     quarter = per // 4
     lane = lax.broadcasted_iota(jnp.int32, (quarter, LANES), 1)
 
@@ -119,7 +125,7 @@
     )(index, displacement)
 
 
-def receive_kernel(per, index_ref, packed_ref, out_ref, rows_ref, block_ref):
+def unpack_rows(per, packed_ref, rows_ref):
     slots = rows_ref.shape[0]
     quarter = per // 4
     lane = lax.broadcasted_iota(jnp.int32, (quarter, LANES), 1)
@@ -138,37 +144,6 @@
         return carry
 
     lax.fori_loop(0, slots // per, peer, 0)
-    chunk = block_ref.shape[0]
-
-    def pick(b, carry):
-        gather_rows(index_ref, rows_ref, block_ref, b * chunk, chunk)
-        at = pl.multiple_of(b * chunk, chunk)
-        out_ref[pl.ds(at, chunk), :] = block_ref[...].astype(jnp.bfloat16)
-        return carry
-
-    lax.fori_loop(0, slots // chunk, pick, 0)
-
-
-def receive_rows(packed, index, per):
-    slots = index.shape[0]
-    return pl.pallas_call(
-        functools.partial(receive_kernel, per),
-        in_specs=[
-            pl.BlockSpec(memory_space=pltpu.SMEM),
-            pl.BlockSpec(memory_space=pltpu.VMEM),
-        ],
-        out_specs=pl.BlockSpec(memory_space=pltpu.VMEM),
-        out_shape=jax.ShapeDtypeStruct((slots, LANES), jnp.bfloat16),
-        scratch_shapes=[
-            pltpu.VMEM((slots, LANES), jnp.float32),
-            pltpu.VMEM((256, LANES), jnp.float32),
-        ],
-        compiler_params=params(32),
-        cost_estimate=pl.CostEstimate(
-            flops=0, bytes_accessed=60 * MIB, transcendentals=0
-        ),
-        name="receive_rows",
-    )(index, packed)
 
 
 def splits(x):
@@ -202,7 +177,7 @@
     return jnp.maximum(1.0 - safe * lax.rsqrt(safe), 0.0)
 
 
-PANEL_CHUNK = 256
+PANEL_CHUNK = 2048
 
 
 def blend_kernel(
@@ -252,9 +227,10 @@
         five = five_ref[pl.ds(first, block_patches), pl.ds(at, PANEL_CHUNK)]
         four = four_ref[pl.ds(first, block_patches), pl.ds(at, PANEL_CHUNK)]
         columns = panel_rows[:, pl.ds(at, PANEL_CHUNK)]
+        whole = jnp.dot(entry_rows, columns, preferred_element_type=jnp.float32)
         for p in range(block_patches):
             rows = slice(p * support_count, (p + 1) * support_count)
-            square = jnp.dot(entry_rows[rows], columns, preferred_element_type=jnp.float32)
+            square = whole[rows]
             u = falloff_terms(square)
             u2 = u * u
             value = u2 * u2 * (five[p : p + 1] - four[p : p + 1] * u)
@@ -295,30 +271,31 @@
     )(points, member.reshape(1, panels), centers.T, support_xyz)
 
 
-def moved_kernel(modes, last, support_count, *refs):
-    if last:
-        inverse_ref, values_ref, blend_ref, start_ref, normals_ref, out_ref = refs[:6]
-        turned_ref, total_ref, coef_ref = refs[6:]
-    else:
-        inverse_ref, values_ref, blend_ref, out_ref = refs[:4]
-        turned_ref, coef_ref = refs[4:]
-        total_ref = out_ref
+BLOCK_PATCHES = 16
+
+
+def moved_kernel(modes, per, support_count, groups, group_ref, index_ref, *refs):
+    packed_ref, blend_ref, normals_ref = refs[:3]
+    inverse_refs = refs[3 : 3 + groups]
+    out_ref, rows_ref, picked_ref, values_ref, turned_ref, coef_ref, total_ref = refs[3 + groups :]
     step = pl.program_id(0)
+    steps = pl.num_programs(0) - 1
+    block = picked_ref.shape[0]
 
     @pl.when(step == 0)
     def _():
-        if last:
-            total_ref[...] = start_ref[...]
-        else:
-            total_ref[...] = jnp.zeros_like(total_ref)
-
-    owners, block_patches, width = inverse_ref.shape
+        total_ref[...] = jnp.zeros_like(total_ref)
+        values_ref[...] = jnp.zeros_like(values_ref)
+        unpack_rows(per, packed_ref, rows_ref)
+
+    block_patches, width = inverse_refs[0].shape
     halves = width // LANES
-    per_patch = owners * halves
-    for o in range(owners):
+    per_patch = groups * halves
+    for k in range(groups):
+        owner = lax.rem(group_ref[0] + groups - k, groups)
         for a in range(halves):
-            piece = inverse_ref[o, :, a * LANES : (a + 1) * LANES].astype(jnp.float32)
-            turned_ref[pl.ds(o * halves + a, block_patches, stride=per_patch), :] = piece
+            piece = inverse_refs[k][:, a * LANES : (a + 1) * LANES].astype(jnp.float32)
+            turned_ref[pl.ds(owner * halves + a, block_patches, stride=per_patch), :] = piece
     lane = lax.broadcasted_iota(jnp.int32, (8, LANES), 1)
     low = lane < support_count
     for pair in range(block_patches // 2):
@@ -331,68 +308,69 @@
                 both = (own, other) if side == 0 else (other, own)
                 keep = low if side == 0 else jnp.logical_not(low)
                 rows += [jnp.where(keep, x, 0.0) for x in both]
-        block = jnp.concatenate(rows, axis=0).astype(jnp.bfloat16)
+        product = jnp.concatenate(rows, axis=0).astype(jnp.bfloat16)
         at = pair * LANES
         coef = jnp.dot(
-            block, values_ref[at : at + LANES, :], preferred_element_type=jnp.float32
+            product, values_ref[at : at + LANES, :], preferred_element_type=jnp.float32
         )
         coef_ref[:, at : at + LANES] = coef.T[: 3 * modes].astype(jnp.bfloat16)
     total_ref[...] += jnp.dot(
         coef_ref[...], blend_ref[...], preferred_element_type=jnp.float32
     )
 
-    if last:
-
-        @pl.when(step == pl.num_programs(0) - 1)
-        def _():
-            result = None
-            for c in range(3):
-                term = normals_ref[c : c + 1, :] * total_ref[c * modes : (c + 1) * modes, :]
-                result = term if result is None else result + term
-            out_ref[...] = result
-
-
-def moved_part(inverse, values, blend, part, modes, support_count, start=None, normals=None):
-    owners, patches, width = inverse.shape
+    base = jnp.minimum(step, steps - 1) * block
+    for r in range(block):
+        picked_ref[r : r + 1, :] = rows_ref[pl.ds(index_ref[base + r], 1), :]
+    values_ref[...] = picked_ref[...].astype(jnp.bfloat16)
+
+    @pl.when(step == steps)
+    def _():
+        result = None
+        for c in range(3):
+            term = normals_ref[c : c + 1, :] * total_ref[c * modes : (c + 1) * modes, :]
+            result = term if result is None else result + term
+        out_ref[...] = result
+
+
+def moved_normals(group, index, packed, per, inverses, blend, normals, modes, support_count):
+    groups = len(inverses)
+    patches, width = inverses[0].shape
     slots, panels = blend.shape
-    block_patches = 16
-    steps = patches // block_patches
-    block = block_patches * support_count
-    last = start is not None
-    in_specs = [
-        pl.BlockSpec((owners, block_patches, width), lambda i: (0, i, 0)),
-        pl.BlockSpec((block, LANES), lambda i: (part * steps + i, 0)),
-        pl.BlockSpec((block, panels), lambda i: (part * steps + i, 0)),
-    ]
-    operands = [inverse, values, blend]
-    total_shape = (3 * modes, panels)
-    scratch = [pltpu.VMEM((block_patches * support_count // 2, LANES), jnp.float32)]
-    if last:
-        in_specs += [
-            pl.BlockSpec(total_shape, lambda i: (0, 0)),
+    steps = patches // BLOCK_PATCHES
+    block = BLOCK_PATCHES * support_count
+
+    def before(i):
+        return jnp.maximum(i - 1, 0)
+
+    return pl.pallas_call(
+        functools.partial(moved_kernel, modes, per, support_count, groups),
+        grid=(steps + 1,),
+        in_specs=[
+            pl.BlockSpec(memory_space=pltpu.SMEM),
+            pl.BlockSpec(memory_space=pltpu.SMEM),
+            pl.BlockSpec(memory_space=pltpu.VMEM),
+            pl.BlockSpec((block, panels), lambda i: (before(i), 0)),
             pl.BlockSpec((3, panels), lambda i: (0, 0)),
         ]
-        operands += [start, normals]
-        scratch += [pltpu.VMEM(total_shape, jnp.float32)]
-        out_shape = (modes, panels)
-    else:
-        out_shape = total_shape
-    scratch += [pltpu.VMEM((3 * modes, block), jnp.bfloat16)]
-    return pl.pallas_call(
-        functools.partial(moved_kernel, modes, last, support_count),
-        grid=(steps,),
-        in_specs=in_specs,
-        out_specs=pl.BlockSpec(out_shape, lambda i: (0, 0)),
-        out_shape=jax.ShapeDtypeStruct(out_shape, jnp.float32),
-        scratch_shapes=scratch,
-        compiler_params=params(40),
+        + [pl.BlockSpec((BLOCK_PATCHES, width), lambda i: (before(i), 0))] * groups,
+        out_specs=pl.BlockSpec((modes, panels), lambda i: (0, 0)),
+        out_shape=jax.ShapeDtypeStruct((modes, panels), jnp.float32),
+        scratch_shapes=[
+            pltpu.VMEM((slots, LANES), jnp.float32),
+            pltpu.VMEM((block, LANES), jnp.float32),
+            pltpu.VMEM((block, LANES), jnp.bfloat16),
+            pltpu.VMEM((block // 2, LANES), jnp.float32),
+            pltpu.VMEM((3 * modes, block), jnp.bfloat16),
+            pltpu.VMEM((3 * modes, panels), jnp.float32),
+        ],
+        compiler_params=params(48),
         cost_estimate=pl.CostEstimate(
-            flops=2 * 3 * modes * panels * patches * support_count,
-            bytes_accessed=2 * panels * patches * support_count,
+            flops=2 * 3 * modes * panels * slots,
+            bytes_accessed=2 * panels * slots,
             transcendentals=0,
         ),
-        name="moved_last" if last else "moved_first",
-    )(*operands)
+        name="moved_normals",
+    )(group.reshape(1), index, packed, blend, normals, *inverses)
 
 
 def shards(
@@ -415,30 +393,34 @@
     support_count = slots // patches
     devices = lax.axis_size(axes)
     per = slots // devices
-    parts = patches // LANES
-
     own_rows = patch_kernel_inverse.shape[0]
     order = inverse_order(own_rows, support_count)
     if not np.array_equal(order, np.arange(support_count)):
         xyz = support_xyz.reshape(3, patches, support_count)
         support_xyz = jnp.take(xyz, order, axis=2).reshape(3, slots)
 
-    def exchange(packed):
-        got = lax.all_to_all(packed, "group", split_axis=0, concat_axis=0, tiled=True)
-        return got
-
-    first = exchange(inverse_pack(patch_kernel_inverse, 0, parts))
-    second_packed = inverse_pack(patch_kernel_inverse, 1, parts)
+    groups = lax.axis_size("group")
+    group = lax.axis_index("group")
+    packs = [
+        inverse_pack(patch_kernel_inverse, lax.rem(group + k, groups), patches)
+        for k in range(groups)
+    ]
+    *packs, displacement = lax.optimization_barrier((*packs, displacement))
+    inverses = [packs[0]]
+    for k in range(1, groups):
+        ring = [(i, (i + k) % groups) for i in range(groups)]
+        inverses.append(lax.ppermute(packs[k], "group", ring))
     outgoing = send_rows(displacement, send_index.reshape(slots), per)
+    outgoing, panel_xyz, inverses[1], inverses[-1] = lax.optimization_barrier(
+        (outgoing, panel_xyz, inverses[1], inverses[-1])
+    )
     arriving = lax.all_to_all(
         outgoing.reshape(devices, per * 3 // 4, LANES), axes, 0, 0, tiled=True
     ).reshape(slots * 3 // 4, LANES)
-    second_packed, _ = lax.optimization_barrier((second_packed, outgoing))
-    second = exchange(second_packed)
     blend = blend_entry_major(panel_xyz, member, support_xyz, centers, support_count)
-    values = receive_rows(arriving, support.reshape(slots), per)
-    total = moved_part(first, values, blend, 0, modes, support_count)
-    return moved_part(second, values, blend, 1, modes, support_count, total, normals)
+    return moved_normals(
+        group, support.reshape(slots), arriving, per, inverses, blend, normals, modes, support_count
+    )
 
 
 def solution(mesh):

time: 294 us -> 183 us (0.62)
  Pallas kernels: 195 us -> 132 us
  waiting for transfers between devices: 66.7 us -> 25.2 us
  starting transfers between devices: 16.7 us -> 12.1 us
    all_to_all x1, waiting for transfers between devices: 66.7 us -> 0.01 us  [shards(): lax.all_to_all(outgoing.reshape(devices, per * 3 // 4, LANES), axes, 0, 0...]
    pallas_call x1, Pallas kernels: 98.5 us -> 66.5 us  [blend_entry_major(): pl.pallas_call(functools.partial(blend_kernel, support_count), grid=(slot...]
    ppermute x0 -> x3, waiting for transfers between devices: none -> 25.2 us  [shards(): inverses.append(lax.ppermute(packs[k], 'group', ring))]
    pallas_call x5, Pallas kernels: 59.5 us -> 39.2 us  [the longest x1 37.3 us: moved_normals(): pl.pallas_call(functools.partial(moved_kernel, modes, per, support_count,...]
    pallas_call x1, Pallas kernels: 37 us -> 25.9 us  [send_rows(): pl.pallas_call(functools.partial(send_kernel, per), in_specs=[pl.BlockSpe...]
    all_to_all x2 -> x0, starting transfers between devices: 10.7 us -> none  [exchange(): lax.all_to_all(packed, 'group', split_axis=0, concat_axis=0, tiled=True)]
    ppermute x0 -> x3, starting transfers between devices: none -> 7.79 us  [shards(): inverses.append(lax.ppermute(packs[k], 'group', ring))]
    unnamed x33 -> x37, local copies, waits for them, and re-layouts: 13.7 us -> 13.2 us
  transfers between devices with their start and end apart: 3 -> 4, of which waited for: 1 -> 1; matrix products, arithmetic and copies ran while one was open for 0% -> 0% of each run, Pallas kernels for 60% -> 51%
where the time goes in v3:
time: 183 us; the launch traced here: 182 us
  Pallas kernels  132 us (72%)
  waiting for transfers between devices  25.2 us (14%)
  local copies, waits for them, and re-layouts  13.2 us (7%)
  starting transfers between devices  12.1 us (7%)
    pallas_call x1, Pallas kernels, blend_entry_major(): pl.pallas_call(functools.partial(blend_kernel, support_count), grid=(slot...  66.5 us
    pallas_call x1, Pallas kernels, moved_normals(): pl.pallas_call(functools.partial(moved_kernel, modes, per, support_count,...  37.3 us
    pallas_call x1, Pallas kernels, send_rows(): pl.pallas_call(functools.partial(send_kernel, per), in_specs=[pl.BlockSpe...  25.9 us
    ppermute x3, waiting for transfers between devices, shards(): inverses.append(lax.ppermute(packs[k], 'group', ring))  25.2 us
    unnamed x37, local copies, waits for them, and re-layouts  13.2 us
    ppermute x3, starting transfers between devices, shards(): inverses.append(lax.ppermute(packs[k], 'group', ring))  7.79 us
    all_to_all x1, starting transfers between devices, shards(): lax.all_to_all(outgoing.reshape(devices, per * 3 // 4, LANES), axes, 0, 0...  4.27 us
  transfers between devices with their start and end apart: 4, of which 1 were waited for; matrix products, arithmetic and copies ran while one was open for 0% of the time, Pallas kernels for 51%

profile of v3, /device:TPU:0, one launch (start us, length us, event | category | flops | bytes accessed | tf_op | source)
XLA Modules:
  0.0 182.1 jit_solution(1990174335437983855)
XLA Ops:
  0.0 0.0 copy-start
  0.0 1.6 copy-done
  1.6 0.0 copy-start.1
  1.6 0.5 inverse_pack.5
  2.1 1.1 copy-done.1
  3.2 0.5 inverse_pack.4.refs_3_
  3.7 0.0 copy-start.4
  3.7 0.8 copy-done.4
  4.4 0.0 copy-start.3
  4.4 0.0 copy-start.12
  4.4 0.5 inverse_pack.7
  4.9 0.5 inverse_pack.6
  5.4 0.0 copy-start.10
  5.4 0.8 copy-done.10
  6.2 3.0 %collective-permute-start = (bf16[256,1024]{1,0:T(8,128)(2,1)S(1)}, bf16[256,1024]{1,0:T(8,128)(2,1)S(1)}, u32[]{:S(2)}, u32[]{:S(2)}) collective-permute-start(bf16[256,1024]{1,0:T(8,128)(2,1)S(1)} %inverse_pack.5), channel_id=1, source_target_pairs={{0,1},{1,2},{2,3},{3,0},{4,5},{5,6},{6,7},{7,4},{8,9},{9,10},{10,1... | collective-permute-start | bytes 1572872 | tf_op jit(solution)/shard_map/ppermute | solution.py:412
  9.2 2.0 %collective-permute-start.1 = (bf16[256,1024]{1,0:T(8,128)(2,1)S(1)}, bf16[256,1024]{1,0:T(8,128)(2,1)S(1)}, u32[]{:S(2)}, u32[]{:S(2)}) collective-permute-start(bf16[256,1024]{1,0:T(8,128)(2,1)S(1)} %inverse_pack.7), channel_id=1, source_target_pairs={{0,3},{1,0},{2,1},{3,2},{4,7},{5,4},{6,5},{7,6},{8,11},{9,8},{10,9... | collective-permute-start | bytes 1572872 | tf_op jit(solution)/shard_map/ppermute | solution.py:412
  11.3 0.0 copy-done.3
  11.3 0.0 copy-done.12
  11.3 25.9 %send_rows.1 = bf16[12288,128]{1,0:T(8,128)(2,1)S(1)} custom-call(s32[16384]{0:T(1024)S(1)} %bitcast.14, bf16[96,16384]{1,0:T(8,128)(2,1)S(1)} %copy-done.3), custom_call_target="tpu_custom_call" | custom-call | bytes 62914560 | tf_op jit(solution)/shard_map/send_rows/pallas_call | solution.py:108
  37.1 0.0 copy-start.2
  37.2 1.7 copy-done.2
  38.8 0.0 collective-permute-done.refs_4_
  38.8 0.0 copy-start.6
  38.8 0.8 copy-done.6
  39.7 0.0 collective-permute-done.1.refs_6_
  39.7 0.0 copy-start.8
  39.7 0.8 copy-done.8
  40.5 0.0 copy-start.17
  40.5 0.0 copy-start.11
  40.5 4.3 %all-to-all-start = ((bf16[32,384,128]{2,1,0:T(8,128)(2,1)}), bf16[32,384,128]{2,1,0:T(8,128)(2,1)S(1)}, u32[]{:S(2)}, u32[]{:S(2)}) async-start(bf16[32,384,128]{2,1,0:T(8,128)(2,1)} %bitcast.12), calls=%async_computation | async-start | bytes 6291456 | tf_op jit(solution)/shard_map/all_to_all | solution.py:417
  44.7 2.7 %collective-permute-start.2 = (bf16[256,1024]{1,0:T(8,128)(2,1)}, bf16[256,1024]{1,0:T(8,128)(2,1)}, u32[]{:S(2)}, u32[]{:S(2)}) collective-permute-start(bf16[256,1024]{1,0:T(8,128)(2,1)} %copy-done.10), channel_id=1, source_target_pairs={{0,2},{1,3},{2,0},{3,1},{4,6},{5,7},{6,4},{7,5},{8,10},{9,11},{10,... | collective-permute-start | bytes 1572872 | tf_op jit(solution)/shard_map/ppermute | solution.py:412
  47.5 0.0 copy-done.17
  47.5 0.1 copy.10
  47.6 0.0 copy-done.11
  47.6 0.0 copy-done.16
  47.6 0.0 copy-start.14
  47.7 0.7 copy-done.14
  48.4 66.5 %blend.1.refs_1_ = bf16[16384,2048]{1,0:T(8,128)(2,1)} custom-call(f32[3,2048]{1,0:T(4,128)S(1)} %copy-done.14, s32[1,2048]{1,0:T(1,128)S(1)} %bitcast.16, f32[256,3]{1,0:T(8,128)S(1)} %bitcast.13, f32[3,16384]{1,0:T(4,128)S(1)} %copy-done.11), custom_call_target="tpu_custom_call" | custom-call | flops 2147483648 | bytes 134217728 | tf_op jit(solution)/shard_map/blend/pallas_call | solution.py:248
  114.9 25.2 %collective-permute-done.2.refs_5_ = bf16[256,1024]{1,0:T(8,128)(2,1)} collective-permute-done((bf16[256,1024]{1,0:T(8,128)(2,1)}, bf16[256,1024]{1,0:T(8,128)(2,1)}, u32[]{:S(2)}, u32[]{:S(2)}) %collective-permute-start.2) | collective-permute-done | bytes 524320 | tf_op jit(solution)/shard_map/ppermute | solution.py:412
  140.1 0.0 all-to-all-done
  140.1 0.0 copy-start.5
  140.1 1.0 copy-done.5
  141.1 1.0 copy-done.7
  142.1 0.0 copy-start.9
  142.2 1.0 copy-done.9
  143.2 0.8 copy-done.13
  144.0 0.8 copy-done.15
  144.8 37.3 %moved_normals.1 = f32[32,2048]{1,0:T(8,128)} custom-call(s32[1]{0:T(128)} %bitcast.group_ref, s32[16384]{0:T(1024)S(1)} %bitcast.15, bf16[12288,128]{1,0:T(8,128)(2,1)S(1)} %bitcast.11, bf16[16384,2048]{1,0:T(8,128)(2,1)} %blend.1.refs_1_, f32[3,2048]{1,0:T(4,128)S(1)} %copy-done.15, bf16[256,1024]{1,0:T(8,128)(2,1)S(1)} %copy-done.5, ...), custom_call_target="tpu_custom_call" | custom-call | flops 6442450944 | bytes 67108864 | tf_op jit(solution)/shard_map/moved_normals/pallas_call | solution.py:345
  (4 shorter events, 0.0 us)
Async XLA Ops:
  0.0 1.6 copy-start
  1.6 1.6 copy-start.1
  3.7 0.8 copy-start.4
  4.4 6.8 %copy-start.3 = (bf16[96,16384]{1,0:T(8,128)(2,1)S(1)}, bf16[96,16384]{1,0:T(8,128)(2,1)}, u32[]{:S(2)}) copy-start(bf16[96,16384]{1,0:T(8,128)(2,1)} %displacement_ref) | copy-start | bytes 9437188
  4.4 6.8 %copy-start.12 = (s32[1,16384]{1,0:T(1,128)S(1)}, s32[1,16384]{1,0:T(1,128)}, u32[]{:S(2)}) copy-start(s32[1,16384]{1,0:T(1,128)} %param.10) | copy-start | bytes 196612
  5.4 0.8 copy-start.10
  6.2 32.6 %collective-permute-start = (bf16[256,1024]{1,0:T(8,128)(2,1)S(1)}, bf16[256,1024]{1,0:T(8,128)(2,1)S(1)}, u32[]{:S(2)}, u32[]{:S(2)}) collective-permute-start(bf16[256,1024]{1,0:T(8,128)(2,1)S(1)} %inverse_pack.5), channel_id=1, source_target_pairs={{0,1},{1,2},{2,3},{3,0},{4,5},{5,6},{6,7},{7,4},{8,9},{9,10},{10,1... | collective-permute-start | bytes 1572872 | tf_op jit(solution)/shard_map/ppermute | solution.py:412
  9.2 30.4 %collective-permute-start.1 = (bf16[256,1024]{1,0:T(8,128)(2,1)S(1)}, bf16[256,1024]{1,0:T(8,128)(2,1)S(1)}, u32[]{:S(2)}, u32[]{:S(2)}) collective-permute-start(bf16[256,1024]{1,0:T(8,128)(2,1)S(1)} %inverse_pack.7), channel_id=1, source_target_pairs={{0,3},{1,0},{2,1},{3,2},{4,7},{5,4},{6,5},{7,6},{8,11},{9,8},{10,9... | collective-permute-start | bytes 1572872 | tf_op jit(solution)/shard_map/ppermute | solution.py:412
  37.1 1.7 copy-start.2
  38.8 0.8 copy-start.6
  39.7 0.8 copy-start.8
  40.5 7.0 %copy-start.17 = (f32[3,256]{1,0:T(4,128)S(1)}, f32[3,256]{1,0:T(4,128)}, u32[]{:S(2)}) copy-start(f32[3,256]{1,0:T(4,128)} %param.16) | copy-start | bytes 9220
  40.5 7.2 %copy-start.11 = (f32[3,16384]{1,0:T(4,128)S(1)}, f32[3,16384]{1,0:T(4,128)}, u32[]{:S(2)}) copy-start(f32[3,16384]{1,0:T(4,128)} %support_ref.1) | copy-start | bytes 589828
  40.5 7.2 %copy-start.16 = (s32[2048]{0:T(1024)S(1)}, s32[2048]{0:T(1024)}, u32[]{:S(2)}) copy-start(s32[2048]{0:T(1024)} %param.17) | copy-start | bytes 24580
  40.5 99.6 %all-to-all-start = ((bf16[32,384,128]{2,1,0:T(8,128)(2,1)}), bf16[32,384,128]{2,1,0:T(8,128)(2,1)S(1)}, u32[]{:S(2)}, u32[]{:S(2)}) async-start(bf16[32,384,128]{2,1,0:T(8,128)(2,1)} %bitcast.12), calls=%async_computation | async-start | bytes 6291456 | tf_op jit(solution)/shard_map/all_to_all | solution.py:417
  44.7 95.3 %collective-permute-start.2 = (bf16[256,1024]{1,0:T(8,128)(2,1)}, bf16[256,1024]{1,0:T(8,128)(2,1)}, u32[]{:S(2)}, u32[]{:S(2)}) collective-permute-start(bf16[256,1024]{1,0:T(8,128)(2,1)} %copy-done.10), channel_id=1, source_target_pairs={{0,2},{1,3},{2,0},{3,1},{4,6},{5,7},{6,4},{7,5},{8,10},{9,11},{10,... | collective-permute-start | bytes 1572872 | tf_op jit(solution)/shard_map/ppermute | solution.py:412
  47.6 0.8 copy-start.14
  140.1 1.0 copy-start.5
  141.1 1.0 copy-start.7
  142.1 1.0 copy-start.9
  143.2 0.8 copy-start.13
  144.0 0.8 copy-start.15

commit v4 on v3

--- a/solution.py
+++ b/solution.py
@@ -178,19 +178,14 @@
 
 
 PANEL_CHUNK = 2048
+SPAN = 16
+EARLY = 1
 
 
 def blend_kernel(
-    support_count,
-    points_ref,
-    member_ref,
-    centers_ref,
-    support_ref,
-    out_ref,
-    panel_rows,
-    five_ref,
-    four_ref,
+    support_count, first_step, points_ref, member_ref, centers_ref, support_ref, *refs
 ):
+    out_ref, panel_rows, five_ref, four_ref = refs[-4:]
     panels = points_ref.shape[1]
     patches = centers_ref.shape[0]
     entries = support_ref.shape[1]
@@ -223,7 +218,7 @@
 
     def chunk(b, carry):
         at = pl.multiple_of(b * PANEL_CHUNK, PANEL_CHUNK)
-        first = pl.multiple_of(step * block_patches, block_patches)
+        first = pl.multiple_of((first_step + step) * block_patches, block_patches)
         five = five_ref[pl.ds(first, block_patches), pl.ds(at, PANEL_CHUNK)]
         four = four_ref[pl.ds(first, block_patches), pl.ds(at, PANEL_CHUNK)]
         columns = panel_rows[:, pl.ds(at, PANEL_CHUNK)]
@@ -240,54 +235,48 @@
     lax.fori_loop(0, panels // PANEL_CHUNK, chunk, 0)
 
 
-def blend_entry_major(points, member, support_xyz, centers, support_count):
+def blend_entry_major(points, member, support_xyz, centers, support_count, span, begun=None):
     panels = points.shape[1]
     patches = centers.shape[1]
     slots = support_xyz.shape[1]
     block = 8 * support_count
+    low, high = (slots * x // (block * SPAN) for x in span)
+    more = [] if begun is None else [begun]
     return pl.pallas_call(
-        functools.partial(blend_kernel, support_count),
-        grid=(slots // block,),
+        functools.partial(blend_kernel, support_count, low),
+        grid=(high - low,),
         in_specs=[
             pl.BlockSpec((3, panels), lambda i: (0, 0)),
             pl.BlockSpec((1, panels), lambda i: (0, 0)),
             pl.BlockSpec((patches, 3), lambda i: (0, 0)),
-            pl.BlockSpec((3, block), lambda i: (0, i)),
-        ],
-        out_specs=pl.BlockSpec((block, panels), lambda i: (i, 0)),
+            pl.BlockSpec((3, block), lambda i: (0, low + i)),
+        ]
+        + [pl.BlockSpec(memory_space=pl.ANY)] * len(more),
+        out_specs=pl.BlockSpec((block, panels), lambda i: (low + i, 0)),
         out_shape=jax.ShapeDtypeStruct((slots, panels), jnp.bfloat16),
         scratch_shapes=[
             pltpu.VMEM((32, panels), jnp.bfloat16),
             pltpu.VMEM((patches, panels), jnp.float32),
             pltpu.VMEM((patches, panels), jnp.float32),
         ],
-        compiler_params=params(40),
+        compiler_params=params(60),
         cost_estimate=pl.CostEstimate(
-            flops=64 * slots * panels,
-            bytes_accessed=4 * slots * panels,
-            transcendentals=slots * panels,
-        ),
+            flops=64 * (high - low) * block * panels,
+            bytes_accessed=4 * (high - low) * block * panels,
+            transcendentals=(high - low) * block * panels,
+        ),
+        input_output_aliases={4: 0} if more else {},
         name="blend",
-    )(points, member.reshape(1, panels), centers.T, support_xyz)
+    )(points, member.reshape(1, panels), centers.T, support_xyz, *more)
 
 
 BLOCK_PATCHES = 16
-
-
-def moved_kernel(modes, per, support_count, groups, group_ref, index_ref, *refs):
-    packed_ref, blend_ref, normals_ref = refs[:3]
-    inverse_refs = refs[3 : 3 + groups]
-    out_ref, rows_ref, picked_ref, values_ref, turned_ref, coef_ref, total_ref = refs[3 + groups :]
-    step = pl.program_id(0)
-    steps = pl.num_programs(0) - 1
-    block = picked_ref.shape[0]
-
-    @pl.when(step == 0)
-    def _():
-        total_ref[...] = jnp.zeros_like(total_ref)
-        values_ref[...] = jnp.zeros_like(values_ref)
-        unpack_rows(per, packed_ref, rows_ref)
-
+BLEND_DEPTH = 6
+
+
+def products_kernel(support_count, groups, group_ref, *refs):
+    inverse_refs = refs[:groups]
+    out_ref, turned_ref = refs[groups:]
     block_patches, width = inverse_refs[0].shape
     halves = width // LANES
     per_patch = groups * halves
@@ -309,21 +298,84 @@
                 keep = low if side == 0 else jnp.logical_not(low)
                 rows += [jnp.where(keep, x, 0.0) for x in both]
         product = jnp.concatenate(rows, axis=0).astype(jnp.bfloat16)
+        out_ref[pair * LANES : (pair + 1) * LANES, :] = product
+
+
+def pair_products(group, inverses, support_count):
+    groups = len(inverses)
+    patches, width = inverses[0].shape
+    block = BLOCK_PATCHES * support_count
+    return pl.pallas_call(
+        functools.partial(products_kernel, support_count, groups),
+        grid=(patches // BLOCK_PATCHES,),
+        in_specs=[pl.BlockSpec(memory_space=pltpu.SMEM)]
+        + [pl.BlockSpec((BLOCK_PATCHES, width), lambda i: (i, 0))] * groups,
+        out_specs=pl.BlockSpec((block, LANES), lambda i: (i, 0)),
+        out_shape=jax.ShapeDtypeStruct((patches * support_count, LANES), jnp.bfloat16),
+        scratch_shapes=[pltpu.VMEM((block // 2, LANES), jnp.float32)],
+        compiler_params=params(60),
+        cost_estimate=pl.CostEstimate(
+            flops=0, bytes_accessed=20 * MIB, transcendentals=0
+        ),
+        name="pair_products",
+    )(group.reshape(1), *inverses)
+
+
+def moved_kernel(modes, per, index_ref, packed_ref, products_ref, blend_ref, normals_ref, *refs):
+    out_ref, rows_ref, picked_ref, values_ref, coef_ref, summed_ref = refs[:6]
+    total_ref, blend_slots, arrived = refs[6:]
+    step = pl.program_id(0)
+    steps = pl.num_programs(0) - 2
+    block = picked_ref.shape[0]
+    depth = blend_slots.shape[0]
+
+    def fetch(b):
+        return pltpu.make_async_copy(
+            blend_ref.at[pl.ds(pl.multiple_of(b * block, block), block), :],
+            blend_slots.at[lax.rem(b, depth)],
+            arrived.at[lax.rem(b, depth)],
+        )
+
+    @pl.when(step == 0)
+    def _():
+        for b in range(depth):
+            fetch(b).start()
+        total_ref[...] = jnp.zeros_like(total_ref)
+        values_ref[...] = jnp.zeros_like(values_ref)
+        coef_ref[...] = jnp.zeros_like(coef_ref)
+        unpack_rows(per, packed_ref, rows_ref)
+        fetch(0).wait()
+
+    @pl.when(step >= 3)
+    def _():
+        fetch(step - 2).wait()
+
+        @pl.when(step - 3 + depth < steps)
+        def _():
+            fetch(step - 3 + depth).start()
+
+    summed_ref[...] = coef_ref[...]
+    slot = lax.rem(jnp.maximum(step - 2, 0), depth)
+    base = jnp.minimum(step, steps - 1) * block
+    pairs = block // LANES
+    tile = total_ref.shape[1] // pairs
+    for pair in range(pairs):
+        columns = slice(pair * tile, (pair + 1) * tile)
+        total_ref[:, columns] += jnp.dot(
+            summed_ref[...], blend_slots[slot, :, columns], preferred_element_type=jnp.float32
+        )
+        for r in range(pair * LANES, (pair + 1) * LANES):
+            picked_ref[r : r + 1, :] = rows_ref[pl.ds(index_ref[base + r], 1), :]
         at = pair * LANES
         coef = jnp.dot(
-            product, values_ref[at : at + LANES, :], preferred_element_type=jnp.float32
+            products_ref[at : at + LANES, :],
+            values_ref[at : at + LANES, :],
+            preferred_element_type=jnp.float32,
         )
         coef_ref[:, at : at + LANES] = coef.T[: 3 * modes].astype(jnp.bfloat16)
-    total_ref[...] += jnp.dot(
-        coef_ref[...], blend_ref[...], preferred_element_type=jnp.float32
-    )
-
-    base = jnp.minimum(step, steps - 1) * block
-    for r in range(block):
-        picked_ref[r : r + 1, :] = rows_ref[pl.ds(index_ref[base + r], 1), :]
     values_ref[...] = picked_ref[...].astype(jnp.bfloat16)
 
-    @pl.when(step == steps)
+    @pl.when(step == steps + 1)
     def _():
         result = None
         for c in range(3):
@@ -332,45 +384,44 @@
         out_ref[...] = result
 
 
-def moved_normals(group, index, packed, per, inverses, blend, normals, modes, support_count):
-    groups = len(inverses)
-    patches, width = inverses[0].shape
+def moved_normals(index, packed, per, products, blend, normals, modes):
     slots, panels = blend.shape
-    steps = patches // BLOCK_PATCHES
-    block = BLOCK_PATCHES * support_count
+    block = BLOCK_PATCHES * (LANES // 2)
+    steps = slots // block
 
     def before(i):
-        return jnp.maximum(i - 1, 0)
+        return jnp.clip(i - 1, 0, steps - 1)
 
     return pl.pallas_call(
-        functools.partial(moved_kernel, modes, per, support_count, groups),
-        grid=(steps + 1,),
+        functools.partial(moved_kernel, modes, per),
+        grid=(steps + 2,),
         in_specs=[
             pl.BlockSpec(memory_space=pltpu.SMEM),
-            pl.BlockSpec(memory_space=pltpu.SMEM),
             pl.BlockSpec(memory_space=pltpu.VMEM),
-            pl.BlockSpec((block, panels), lambda i: (before(i), 0)),
+            pl.BlockSpec((block, LANES), lambda i: (before(i), 0)),
+            pl.BlockSpec(memory_space=pl.ANY),
             pl.BlockSpec((3, panels), lambda i: (0, 0)),
-        ]
-        + [pl.BlockSpec((BLOCK_PATCHES, width), lambda i: (before(i), 0))] * groups,
+        ],
         out_specs=pl.BlockSpec((modes, panels), lambda i: (0, 0)),
         out_shape=jax.ShapeDtypeStruct((modes, panels), jnp.float32),
         scratch_shapes=[
             pltpu.VMEM((slots, LANES), jnp.float32),
             pltpu.VMEM((block, LANES), jnp.float32),
             pltpu.VMEM((block, LANES), jnp.bfloat16),
-            pltpu.VMEM((block // 2, LANES), jnp.float32),
+            pltpu.VMEM((3 * modes, block), jnp.bfloat16),
             pltpu.VMEM((3 * modes, block), jnp.bfloat16),
             pltpu.VMEM((3 * modes, panels), jnp.float32),
+            pltpu.VMEM((BLEND_DEPTH, block, panels), jnp.bfloat16),
+            pltpu.SemaphoreType.DMA((BLEND_DEPTH,)),
         ],
-        compiler_params=params(48),
+        compiler_params=params(60),
         cost_estimate=pl.CostEstimate(
             flops=2 * 3 * modes * panels * slots,
             bytes_accessed=2 * panels * slots,
             transcendentals=0,
         ),
         name="moved_normals",
-    )(group.reshape(1), index, packed, blend, normals, *inverses)
+    )(index, packed, products, blend, normals)
 
 
 def shards(
@@ -405,21 +456,21 @@
         inverse_pack(patch_kernel_inverse, lax.rem(group + k, groups), patches)
         for k in range(groups)
     ]
-    *packs, displacement = lax.optimization_barrier((*packs, displacement))
     inverses = [packs[0]]
     for k in range(1, groups):
         ring = [(i, (i + k) % groups) for i in range(groups)]
         inverses.append(lax.ppermute(packs[k], "group", ring))
     outgoing = send_rows(displacement, send_index.reshape(slots), per)
-    outgoing, panel_xyz, inverses[1], inverses[-1] = lax.optimization_barrier(
-        (outgoing, panel_xyz, inverses[1], inverses[-1])
-    )
+    shape = (panel_xyz, member, support_xyz, centers)
+    blend = blend_entry_major(*shape, support_count, (0, EARLY))
+    outgoing, blend, inverses = lax.optimization_barrier((outgoing, blend, inverses))
     arriving = lax.all_to_all(
         outgoing.reshape(devices, per * 3 // 4, LANES), axes, 0, 0, tiled=True
     ).reshape(slots * 3 // 4, LANES)
-    blend = blend_entry_major(panel_xyz, member, support_xyz, centers, support_count)
+    products = pair_products(group, inverses, support_count)
+    blend = blend_entry_major(*shape, support_count, (EARLY, SPAN), blend)
     return moved_normals(
-        group, support.reshape(slots), arriving, per, inverses, blend, normals, modes, support_count
+        support.reshape(slots), arriving, per, products, blend, normals, modes
     )
 
 

time: 183 us -> 168 us (0.918)
  waiting for transfers between devices: 25.2 us -> 0.01 us
  Pallas kernels: 132 us -> 149 us
  local copies, waits for them, and re-layouts: 13.2 us -> 6.73 us
    ppermute x3, waiting for transfers between devices: 25.2 us -> 0.01 us  [shards(): inverses.append(lax.ppermute(packs[k], 'group', ring))]
    pallas_call x2 -> x4, Pallas kernels: 104 us -> 119 us  [the longest x2 74.5 us: blend_entry_major(): pl.pallas_call(functools.partial(blend_kernel, support_count, low), grid=...]
    unnamed x37 -> x15, local copies, waits for them, and re-layouts: 13.2 us -> 6.73 us
  transfers between devices with their start and end apart: 4 -> 4, of which waited for: 1 -> 0; matrix products, arithmetic and copies ran while one was open for 0% -> 0% of each run, Pallas kernels for 51% -> 69%
where the time goes in v4:
time: 168 us; the launch traced here: 167 us
  Pallas kernels  149 us (89%)
  starting transfers between devices  11.2 us (7%)
  local copies, waits for them, and re-layouts  6.73 us (4%)
    pallas_call x2, Pallas kernels, blend_entry_major(): pl.pallas_call(functools.partial(blend_kernel, support_count, low), grid=...  74.5 us
    pallas_call x1, Pallas kernels, moved_normals(): pl.pallas_call(functools.partial(moved_kernel, modes, per), grid=(steps +...  33.5 us
    pallas_call x1, Pallas kernels, send_rows(): pl.pallas_call(functools.partial(send_kernel, per), in_specs=[pl.BlockSpe...  27.5 us
    pallas_call x1, Pallas kernels, pair_products(): pl.pallas_call(functools.partial(products_kernel, support_count, groups),...  10.7 us
    ppermute x3, starting transfers between devices, shards(): inverses.append(lax.ppermute(packs[k], 'group', ring))  7.08 us
    unnamed x15, local copies, waits for them, and re-layouts  6.73 us
    all_to_all x1, starting transfers between devices, shards(): lax.all_to_all(outgoing.reshape(devices, per * 3 // 4, LANES), axes, 0, 0...  4.1 us
  transfers between devices with their start and end apart: 4, of which 0 were waited for; matrix products, arithmetic and copies ran while one was open for 0% of the time, Pallas kernels for 69%

profile of v4, /device:TPU:0, one launch (start us, length us, event | category | flops | bytes accessed | tf_op | source)
XLA Modules:
  0.0 166.7 jit_solution(15815023061712466815)
XLA Ops:
  0.0 0.0 copy-start
  0.0 1.6 copy-done
  1.6 0.0 copy-start.1
  1.6 0.5 inverse_pack.5
  2.1 3.1 %collective-permute-start = (bf16[256,1024]{1,0:T(8,128)(2,1)S(1)}, bf16[256,1024]{1,0:T(8,128)(2,1)}, u32[]{:S(2)}, u32[]{:S(2)}) collective-permute-start(bf16[256,1024]{1,0:T(8,128)(2,1)S(1)} %inverse_pack.5), channel_id=1, source_target_pairs={{0,1},{1,2},{2,3},{3,0},{4,5},{5,6},{6,7},{7,4},{8,9},{9,10},{10,1... | collective-permute-start | bytes 1572872 | tf_op jit(solution)/shard_map/ppermute | solution.py:462
  5.1 0.0 copy-done.1
  5.1 0.5 inverse_pack.6
  5.6 0.0 copy-start.6
  5.6 0.0 copy-start.4
  5.6 2.7 %collective-permute-start.1 = (bf16[256,1024]{1,0:T(8,128)(2,1)S(1)}, bf16[256,1024]{1,0:T(8,128)(2,1)}, u32[]{:S(2)}, u32[]{:S(2)}) collective-permute-start(bf16[256,1024]{1,0:T(8,128)(2,1)S(1)} %inverse_pack.6), channel_id=1, source_target_pairs={{0,2},{1,3},{2,0},{3,1},{4,6},{5,7},{6,4},{7,5},{8,10},{9,11},{10,... | collective-permute-start | bytes 1572872 | tf_op jit(solution)/shard_map/ppermute | solution.py:462
  8.3 1.2 inverse_pack.7
  9.5 1.3 collective-permute-start.2
  10.8 0.5 inverse_pack.4.refs_0_
  11.3 0.0 copy-start.3
  11.3 0.8 copy-done.3
  12.1 0.0 copy-done.6
  12.1 0.8 copy.11
  12.9 0.0 copy-done.4
  12.9 0.0 copy-start.2
  12.9 1.9 %copy-done.2 = bf16[96,16384]{1,0:T(8,128)(2,1)S(1)} copy-done((bf16[96,16384]{1,0:T(8,128)(2,1)S(1)}, bf16[96,16384]{1,0:T(8,128)(2,1)}, u32[]{:S(2)}) %copy-start.2) | copy-done | bytes 3145752
  14.8 27.5 %send_rows.1 = bf16[12288,128]{1,0:T(8,128)(2,1)} custom-call(s32[16384]{0:T(1024)S(1)} %bitcast.11, bf16[96,16384]{1,0:T(8,128)(2,1)S(1)} %copy-done.2), custom_call_target="tpu_custom_call" | custom-call | bytes 62914560 | tf_op jit(solution)/shard_map/send_rows/pallas_call | solution.py:108
  42.3 10.4 %blend.2.refs_0_ = bf16[16384,2048]{1,0:T(8,128)(2,1)} custom-call(f32[3,2048]{1,0:T(4,128)} %points_ref.3, s32[1,2048]{1,0:T(1,128)} %bitcast.16, f32[256,3]{1,0:T(8,128)} %bitcast.13, f32[3,16384]{1,0:T(4,128)} %support_ref.3), custom_call_target="tpu_custom_call" | custom-call | flops 134217728 | bytes 8388608 | tf_op jit(solution)/shard_map/blend/pallas_call | solution.py:245
  52.7 0.0 collective-permute-done.refs_1_
  52.7 0.0 collective-permute-done.1.refs_2_
  52.7 0.0 collective-permute-done.2.refs_3_
  52.7 4.1 %all-to-all-start = ((bf16[32,384,128]{2,1,0:T(8,128)(2,1)}), bf16[32,384,128]{2,1,0:T(8,128)(2,1)S(1)}, u32[]{:S(2)}, u32[]{:S(2)}) async-start(bf16[32,384,128]{2,1,0:T(8,128)(2,1)} %bitcast.8), calls=%async_computation | async-start | bytes 6291456 | tf_op jit(solution)/shard_map/all_to_all | solution.py:467
  56.8 10.7 %pair_products.1.products_ref = bf16[16384,128]{1,0:T(8,128)(2,1)} custom-call(s32[1]{0:T(128)} %bitcast.10.group_ref, bf16[256,1024]{1,0:T(8,128)(2,1)} %copy-done.3, bf16[256,1024]{1,0:T(8,128)(2,1)} %collective-permute-done.refs_1_, bf16[256,1024]{1,0:T(8,128)(2,1)} %collective-permute-done.1.refs_2_, bf16[256,1024]{1,0:T(8,128)(2,1)} %collective-permute-done.2.refs_3_), custom_call_target="tpu_custom_call" | custom-call | bytes 20971520 | tf_op jit(solution)/shard_map/pair_products/pallas_call | solution.py:308
  67.5 64.1 %blend.3.blend_ref = bf16[16384,2048]{1,0:T(8,128)(2,1)} custom-call(f32[3,2048]{1,0:T(4,128)} %points_ref.3, s32[1,2048]{1,0:T(1,128)} %bitcast.17, f32[256,3]{1,0:T(8,128)} %bitcast.14, f32[3,16384]{1,0:T(4,128)} %support_ref.3, bf16[16384,2048]{1,0:T(8,128)(2,1)} %blend.2.refs_0_), custom_call_target="tpu_custom_call", output_to_operand_aliasing={{}: (4, {})} | custom-call | flops 2013265920 | bytes 125829120 | tf_op jit(solution)/shard_map/blend/pallas_call | solution.py:245
  131.6 0.0 all-to-all-done
  131.6 0.0 copy-start.5
  131.6 1.6 copy-done.5
  133.2 33.5 %moved_normals.1 = f32[32,2048]{1,0:T(8,128)} custom-call(s32[16384]{0:T(1024)} %bitcast.15, bf16[12288,128]{1,0:T(8,128)(2,1)} %bitcast.12, bf16[16384,128]{1,0:T(8,128)(2,1)} %pair_products.1.products_ref, bf16[16384,2048]{1,0:T(8,128)(2,1)} %blend.3.blend_ref, f32[3,2048]{1,0:T(4,128)} %normals_ref.1), custom_call_target="tpu_custom_call" | custom-call | flops 6442450944 | bytes 67108864 | tf_op jit(solution)/shard_map/moved_normals/pallas_call | solution.py:395
Async XLA Ops:
  0.0 1.6 copy-start
  1.6 3.6 %copy-start.1 = (bf16[16,64,1024]{2,1,0:T(8,128)(2,1)S(1)}, bf16[16,64,1024]{2,1,0:T(8,128)(2,1)}, u32[]{:S(2)}) copy-start(bf16[16,64,1024]{2,1,0:T(8,128)(2,1)} %inverse_ref.7) | copy-start | bytes 6291460
  2.1 50.6 %collective-permute-start = (bf16[256,1024]{1,0:T(8,128)(2,1)S(1)}, bf16[256,1024]{1,0:T(8,128)(2,1)}, u32[]{:S(2)}, u32[]{:S(2)}) collective-permute-start(bf16[256,1024]{1,0:T(8,128)(2,1)S(1)} %inverse_pack.5), channel_id=1, source_target_pairs={{0,1},{1,2},{2,3},{3,0},{4,5},{5,6},{6,7},{7,4},{8,9},{9,10},{10,1... | collective-permute-start | bytes 1572872 | tf_op jit(solution)/shard_map/ppermute | solution.py:462
  5.6 6.5 %copy-start.6 = (f32[3,256]{1,0:T(4,128)S(1)}, f32[3,256]{1,0:T(4,128)}, u32[]{:S(2)}) copy-start(f32[3,256]{1,0:T(4,128)} %param.16) | copy-start | bytes 9220
  5.6 7.3 %copy-start.4 = (s32[1,16384]{1,0:T(1,128)S(1)}, s32[1,16384]{1,0:T(1,128)}, u32[]{:S(2)}) copy-start(s32[1,16384]{1,0:T(1,128)} %param.10) | copy-start | bytes 196612
  5.6 47.0 %collective-permute-start.1 = (bf16[256,1024]{1,0:T(8,128)(2,1)S(1)}, bf16[256,1024]{1,0:T(8,128)(2,1)}, u32[]{:S(2)}, u32[]{:S(2)}) collective-permute-start(bf16[256,1024]{1,0:T(8,128)(2,1)S(1)} %inverse_pack.6), channel_id=1, source_target_pairs={{0,2},{1,3},{2,0},{3,1},{4,6},{5,7},{6,4},{7,5},{8,10},{9,11},{10,... | collective-permute-start | bytes 1572872 | tf_op jit(solution)/shard_map/ppermute | solution.py:462
  9.5 43.2 %collective-permute-start.2 = (bf16[256,1024]{1,0:T(8,128)(2,1)}, bf16[256,1024]{1,0:T(8,128)(2,1)}, u32[]{:S(2)}, u32[]{:S(2)}) collective-permute-start(bf16[256,1024]{1,0:T(8,128)(2,1)} %inverse_pack.7), channel_id=1, source_target_pairs={{0,3},{1,0},{2,1},{3,2},{4,7},{5,4},{6,5},{7,6},{8,11},{9,8},{10,9... | collective-permute-start | bytes 1572872 | tf_op jit(solution)/shard_map/ppermute | solution.py:462
  11.3 0.8 copy-start.3
  12.9 1.9 %copy-start.2 = (bf16[96,16384]{1,0:T(8,128)(2,1)S(1)}, bf16[96,16384]{1,0:T(8,128)(2,1)}, u32[]{:S(2)}) copy-start(bf16[96,16384]{1,0:T(8,128)(2,1)} %displacement_ref.1) | copy-start | bytes 9437188
  52.7 78.9 %all-to-all-start = ((bf16[32,384,128]{2,1,0:T(8,128)(2,1)}), bf16[32,384,128]{2,1,0:T(8,128)(2,1)S(1)}, u32[]{:S(2)}, u32[]{:S(2)}) async-start(bf16[32,384,128]{2,1,0:T(8,128)(2,1)} %bitcast.8), calls=%async_computation | async-start | bytes 6291456 | tf_op jit(solution)/shard_map/all_to_all | solution.py:467
  131.6 1.6 copy-start.5

commit v5 on v4

--- a/solution.py
+++ b/solution.py
@@ -64,6 +64,7 @@
 
 
 UNROLL = 128
+PIECES = 4
 
 
 def gather_rows(index_ref, source, target, base, count):
@@ -76,8 +77,20 @@
     lax.fori_loop(0, count // UNROLL, body, 0)
 
 
-def send_kernel(per, index_ref, displacement_ref, out_ref, rows_ref, block_ref):
+def send_kernel(
+    per, index_ref, source_ref, out_ref, rows_ref, block_ref, displacement_ref, arrived
+):
     columns, nodes = displacement_ref.shape
+    piece_nodes = nodes // PIECES
+
+    def fetch(i):
+        span = pl.ds(i * piece_nodes, piece_nodes)
+        return pltpu.make_async_copy(
+            source_ref.at[:, span], displacement_ref.at[:, span], arrived.at[i]
+        )
+
+    for i in range(PIECES):
+        fetch(i).start()
 
     def turn(block, carry):
         at = pl.multiple_of(block * LANES, LANES)
@@ -86,7 +99,10 @@
         rows_ref[pl.ds(at, LANES), :] = piece.T
         return carry
 
-    lax.fori_loop(0, nodes // LANES, turn, 0, unroll=4)
+    blocks = piece_nodes // LANES
+    for i in range(PIECES):
+        fetch(i).wait()
+        lax.fori_loop(i * blocks, (i + 1) * blocks, turn, 0, unroll=4)
     quarter = per // 4
     lane = lax.broadcasted_iota(jnp.int32, (quarter, LANES), 1)
 
@@ -109,15 +125,17 @@
         functools.partial(send_kernel, per),
         in_specs=[
             pl.BlockSpec(memory_space=pltpu.SMEM),
-            pl.BlockSpec(memory_space=pltpu.VMEM),
+            pl.BlockSpec(memory_space=pl.ANY),
         ],
         out_specs=pl.BlockSpec(memory_space=pltpu.VMEM),
         out_shape=jax.ShapeDtypeStruct((nodes * 3 // 4, LANES), jnp.bfloat16),
         scratch_shapes=[
             pltpu.VMEM((nodes, LANES), jnp.float32),
             pltpu.VMEM((per, LANES), jnp.float32),
-        ],
-        compiler_params=params(32),
+            pltpu.VMEM((columns, nodes), jnp.bfloat16),
+            pltpu.SemaphoreType.DMA((PIECES,)),
+        ],
+        compiler_params=params(56),
         cost_estimate=pl.CostEstimate(
             flops=0, bytes_accessed=60 * MIB, transcendentals=0
         ),
@@ -125,8 +143,7 @@
     )(index, displacement)
 
 
-def unpack_rows(per, packed_ref, rows_ref):
-    slots = rows_ref.shape[0]
+def unpack_rows(per, packed_ref, rows_ref, first, end):
     quarter = per // 4
     lane = lax.broadcasted_iota(jnp.int32, (quarter, LANES), 1)
 
@@ -143,7 +160,7 @@
         rows_ref[pl.ds(to, quarter), :] = last
         return carry
 
-    lax.fori_loop(0, slots // per, peer, 0)
+    lax.fori_loop(first, end, peer, 0)
 
 
 def splits(x):
@@ -178,49 +195,72 @@
 
 
 PANEL_CHUNK = 2048
-SPAN = 16
-EARLY = 1
-
-
-def blend_kernel(
-    support_count, first_step, points_ref, member_ref, centers_ref, support_ref, *refs
-):
-    out_ref, panel_rows, five_ref, four_ref = refs[-4:]
+
+
+def weights_kernel(points_ref, member_ref, centers_ref, five_ref, four_ref):
     panels = points_ref.shape[1]
     patches = centers_ref.shape[0]
-    entries = support_ref.shape[1]
-    block_patches = entries // support_count
-    step = pl.program_id(0)
-
-    @pl.when(step == 0)
+    patch = lax.broadcasted_iota(jnp.int32, (patches, LANES), 0)
+
+    def weigh(b, carry):
+        at = pl.multiple_of(b * LANES, LANES)
+        square = None
+        for c in range(3):
+            gap = centers_ref[:, c : c + 1] - points_ref[c : c + 1, pl.ds(at, LANES)]
+            square = gap * gap if square is None else square + gap * gap
+        u = falloff_terms(square * (1.0 / ATTRACTION_REACH**2))
+        u2 = u * u
+        owner = jnp.where(member_ref[:, pl.ds(at, LANES)] == patch, OWNER_PREMIUM, 0.0)
+        attraction = u2 * u2 * (5.0 - 4.0 * u) + owner
+        weight = attraction / jnp.sum(attraction, axis=0, keepdims=True)
+        five_ref[:, pl.ds(at, LANES)] = 5.0 * weight
+        four_ref[:, pl.ds(at, LANES)] = 4.0 * weight
+        return carry
+
+    lax.fori_loop(0, panels // LANES, weigh, 0, unroll=2)
+
+
+def panel_weights(points, member, centers):
+    panels = points.shape[1]
+    patches = centers.shape[1]
+    tile = panels // 4
+    shape = jax.ShapeDtypeStruct((patches, panels), jnp.float32)
+    return pl.pallas_call(
+        weights_kernel,
+        grid=(panels // tile,),
+        in_specs=[
+            pl.BlockSpec((3, tile), lambda i: (0, i)),
+            pl.BlockSpec((1, tile), lambda i: (0, i)),
+            pl.BlockSpec((patches, 3), lambda i: (0, 0)),
+        ],
+        out_specs=[pl.BlockSpec((patches, tile), lambda i: (0, i))] * 2,
+        out_shape=(shape, shape),
+        compiler_params=params(60),
+        cost_estimate=pl.CostEstimate(
+            flops=20 * patches * panels,
+            bytes_accessed=8 * patches * panels,
+            transcendentals=patches * panels,
+        ),
+        name="panel_weights",
+    )(points, member.reshape(1, panels), centers.T)
+
+
+def blend_kernel(
+    support_count, points_ref, five_ref, four_ref, support_ref, out_ref, panel_rows
+):
+    panels = points_ref.shape[1]
+    block_patches = five_ref.shape[0]
+
+    @pl.when(pl.program_id(0) == 0)
     def _():
         panel_rows[...] = distance_rows(points_ref[...], False).astype(jnp.bfloat16)
-        patch = lax.broadcasted_iota(jnp.int32, (patches, LANES), 0)
-
-        def weigh(b, carry):
-            at = pl.multiple_of(b * LANES, LANES)
-            square = None
-            for c in range(3):
-                gap = centers_ref[:, c : c + 1] - points_ref[c : c + 1, pl.ds(at, LANES)]
-                square = gap * gap if square is None else square + gap * gap
-            u = falloff_terms(square * (1.0 / ATTRACTION_REACH**2))
-            u2 = u * u
-            owner = jnp.where(member_ref[:, pl.ds(at, LANES)] == patch, OWNER_PREMIUM, 0.0)
-            attraction = u2 * u2 * (5.0 - 4.0 * u) + owner
-            weight = attraction / jnp.sum(attraction, axis=0, keepdims=True)
-            five_ref[:, pl.ds(at, LANES)] = 5.0 * weight
-            four_ref[:, pl.ds(at, LANES)] = 4.0 * weight
-            return carry
-
-        lax.fori_loop(0, panels // LANES, weigh, 0)
 
     entry_rows = distance_rows(support_ref[...], True).T.astype(jnp.bfloat16)
 
     def chunk(b, carry):
         at = pl.multiple_of(b * PANEL_CHUNK, PANEL_CHUNK)
-        first = pl.multiple_of((first_step + step) * block_patches, block_patches)
-        five = five_ref[pl.ds(first, block_patches), pl.ds(at, PANEL_CHUNK)]
-        four = four_ref[pl.ds(first, block_patches), pl.ds(at, PANEL_CHUNK)]
+        five = five_ref[:, pl.ds(at, PANEL_CHUNK)]
+        four = four_ref[:, pl.ds(at, PANEL_CHUNK)]
         columns = panel_rows[:, pl.ds(at, PANEL_CHUNK)]
         whole = jnp.dot(entry_rows, columns, preferred_element_type=jnp.float32)
         for p in range(block_patches):
@@ -235,43 +275,37 @@
     lax.fori_loop(0, panels // PANEL_CHUNK, chunk, 0)
 
 
-def blend_entry_major(points, member, support_xyz, centers, support_count, span, begun=None):
+def blend_entry_major(points, weights, support_xyz, support_count):
     panels = points.shape[1]
-    patches = centers.shape[1]
     slots = support_xyz.shape[1]
     block = 8 * support_count
-    low, high = (slots * x // (block * SPAN) for x in span)
-    more = [] if begun is None else [begun]
     return pl.pallas_call(
-        functools.partial(blend_kernel, support_count, low),
-        grid=(high - low,),
+        functools.partial(blend_kernel, support_count),
+        grid=(slots // block,),
         in_specs=[
             pl.BlockSpec((3, panels), lambda i: (0, 0)),
-            pl.BlockSpec((1, panels), lambda i: (0, 0)),
-            pl.BlockSpec((patches, 3), lambda i: (0, 0)),
-            pl.BlockSpec((3, block), lambda i: (0, low + i)),
-        ]
-        + [pl.BlockSpec(memory_space=pl.ANY)] * len(more),
-        out_specs=pl.BlockSpec((block, panels), lambda i: (low + i, 0)),
+            pl.BlockSpec((8, panels), lambda i: (i, 0)),
+            pl.BlockSpec((8, panels), lambda i: (i, 0)),
+            pl.BlockSpec((3, block), lambda i: (0, i)),
+        ],
+        out_specs=pl.BlockSpec((block, panels), lambda i: (i, 0)),
         out_shape=jax.ShapeDtypeStruct((slots, panels), jnp.bfloat16),
         scratch_shapes=[
             pltpu.VMEM((32, panels), jnp.bfloat16),
-            pltpu.VMEM((patches, panels), jnp.float32),
-            pltpu.VMEM((patches, panels), jnp.float32),
         ],
         compiler_params=params(60),
         cost_estimate=pl.CostEstimate(
-            flops=64 * (high - low) * block * panels,
-            bytes_accessed=4 * (high - low) * block * panels,
-            transcendentals=(high - low) * block * panels,
-        ),
-        input_output_aliases={4: 0} if more else {},
+            flops=64 * slots * panels,
+            bytes_accessed=4 * slots * panels,
+            transcendentals=slots * panels,
+        ),
         name="blend",
-    )(points, member.reshape(1, panels), centers.T, support_xyz, *more)
+    )(points, *weights, support_xyz)
 
 
 BLOCK_PATCHES = 16
-BLEND_DEPTH = 6
+BLEND_DEPTH = 4
+PRODUCT_PATCHES = 64
 
 
 def products_kernel(support_count, groups, group_ref, *refs):
@@ -304,12 +338,12 @@
 def pair_products(group, inverses, support_count):
     groups = len(inverses)
     patches, width = inverses[0].shape
-    block = BLOCK_PATCHES * support_count
+    block = PRODUCT_PATCHES * support_count
     return pl.pallas_call(
         functools.partial(products_kernel, support_count, groups),
-        grid=(patches // BLOCK_PATCHES,),
+        grid=(patches // PRODUCT_PATCHES,),
         in_specs=[pl.BlockSpec(memory_space=pltpu.SMEM)]
-        + [pl.BlockSpec((BLOCK_PATCHES, width), lambda i: (i, 0))] * groups,
+        + [pl.BlockSpec((PRODUCT_PATCHES, width), lambda i: (i, 0))] * groups,
         out_specs=pl.BlockSpec((block, LANES), lambda i: (i, 0)),
         out_shape=jax.ShapeDtypeStruct((patches * support_count, LANES), jnp.bfloat16),
         scratch_shapes=[pltpu.VMEM((block // 2, LANES), jnp.float32)],
@@ -321,9 +355,9 @@
     )(group.reshape(1), *inverses)
 
 
-def moved_kernel(modes, per, index_ref, packed_ref, products_ref, blend_ref, normals_ref, *refs):
+def moved_kernel(modes, per, index_ref, source_ref, products_ref, blend_ref, normals_ref, *refs):
     out_ref, rows_ref, picked_ref, values_ref, coef_ref, summed_ref = refs[:6]
-    total_ref, blend_slots, arrived = refs[6:]
+    total_ref, blend_slots, arrived, packed_ref, landed = refs[6:]
     step = pl.program_id(0)
     steps = pl.num_programs(0) - 2
     block = picked_ref.shape[0]
@@ -338,12 +372,23 @@
 
     @pl.when(step == 0)
     def _():
+        rows = packed_ref.shape[0] // PIECES
+        pieces = []
+        for i in range(PIECES):
+            span = pl.ds(i * rows, rows)
+            pieces.append(
+                pltpu.make_async_copy(source_ref.at[span], packed_ref.at[span], landed.at[i])
+            )
+            pieces[i].start()
         for b in range(depth):
             fetch(b).start()
         total_ref[...] = jnp.zeros_like(total_ref)
         values_ref[...] = jnp.zeros_like(values_ref)
         coef_ref[...] = jnp.zeros_like(coef_ref)
-        unpack_rows(per, packed_ref, rows_ref)
+        peers = rows_ref.shape[0] // (per * PIECES)
+        for i in range(PIECES):
+            pieces[i].wait()
+            unpack_rows(per, packed_ref, rows_ref, i * peers, (i + 1) * peers)
         fetch(0).wait()
 
     @pl.when(step >= 3)
@@ -397,7 +442,7 @@
         grid=(steps + 2,),
         in_specs=[
             pl.BlockSpec(memory_space=pltpu.SMEM),
-            pl.BlockSpec(memory_space=pltpu.VMEM),
+            pl.BlockSpec(memory_space=pl.ANY),
             pl.BlockSpec((block, LANES), lambda i: (before(i), 0)),
             pl.BlockSpec(memory_space=pl.ANY),
             pl.BlockSpec((3, panels), lambda i: (0, 0)),
@@ -413,6 +458,8 @@
             pltpu.VMEM((3 * modes, panels), jnp.float32),
             pltpu.VMEM((BLEND_DEPTH, block, panels), jnp.bfloat16),
             pltpu.SemaphoreType.DMA((BLEND_DEPTH,)),
+            pltpu.VMEM(packed.shape, jnp.bfloat16),
+            pltpu.SemaphoreType.DMA((PIECES,)),
         ],
         compiler_params=params(60),
         cost_estimate=pl.CostEstimate(
@@ -461,14 +508,13 @@
         ring = [(i, (i + k) % groups) for i in range(groups)]
         inverses.append(lax.ppermute(packs[k], "group", ring))
     outgoing = send_rows(displacement, send_index.reshape(slots), per)
-    shape = (panel_xyz, member, support_xyz, centers)
-    blend = blend_entry_major(*shape, support_count, (0, EARLY))
-    outgoing, blend, inverses = lax.optimization_barrier((outgoing, blend, inverses))
+    weights = panel_weights(panel_xyz, member, centers)
+    outgoing, weights, inverses = lax.optimization_barrier((outgoing, weights, inverses))
     arriving = lax.all_to_all(
         outgoing.reshape(devices, per * 3 // 4, LANES), axes, 0, 0, tiled=True
     ).reshape(slots * 3 // 4, LANES)
     products = pair_products(group, inverses, support_count)
-    blend = blend_entry_major(*shape, support_count, (EARLY, SPAN), blend)
+    blend = blend_entry_major(panel_xyz, weights, support_xyz, support_count)
     return moved_normals(
         support.reshape(slots), arriving, per, products, blend, normals, modes
     )

time: 168 us -> 161 us (0.958)
  Pallas kernels: 149 us -> 139 us
  starting transfers between devices: 11.2 us -> 16.6 us
  local copies, waits for them, and re-layouts: 6.73 us -> 4.86 us
    all_to_all x1, starting transfers between devices: 4.1 us -> 9.57 us  [shards(): lax.all_to_all(outgoing.reshape(devices, per * 3 // 4, LANES), axes, 0, 0...]
    pallas_call x2, Pallas kernels: 74.5 us -> 69.3 us  [the longest x1 63.8 us: blend_entry_major(): pl.pallas_call(functools.partial(blend_kernel, support_count), grid=(slot...]
    pallas_call x1, Pallas kernels: 10.7 us -> 6.01 us  [pair_products(): pl.pallas_call(functools.partial(products_kernel, support_count, groups),...]
    unnamed x15 -> x11, local copies, waits for them, and re-layouts: 6.73 us -> 4.86 us
  transfers between devices with their start and end apart: 4 -> 4, of which waited for: 0 -> 1; matrix products, arithmetic and copies ran while one was open for 0% -> 0% of each run, Pallas kernels for 69% -> 66%
where the time goes in v5:
time: 161 us; the launch traced here: 160 us
  Pallas kernels  139 us (86%)
  starting transfers between devices  16.6 us (10%)
  local copies, waits for them, and re-layouts  4.86 us (3%)
    pallas_call x1, Pallas kernels, blend_entry_major(): pl.pallas_call(functools.partial(blend_kernel, support_count), grid=(slot...  63.8 us
    pallas_call x1, Pallas kernels, moved_normals(): pl.pallas_call(functools.partial(moved_kernel, modes, per), grid=(steps +...  31.9 us
    pallas_call x1, Pallas kernels, send_rows(): pl.pallas_call(functools.partial(send_kernel, per), in_specs=[pl.BlockSpe...  28.8 us
    all_to_all x1, starting transfers between devices, shards(): lax.all_to_all(outgoing.reshape(devices, per * 3 // 4, LANES), axes, 0, 0...  9.57 us
    ppermute x3, starting transfers between devices, shards(): inverses.append(lax.ppermute(packs[k], 'group', ring))  7.08 us
    pallas_call x1, Pallas kernels, pair_products(): pl.pallas_call(functools.partial(products_kernel, support_count, groups),...  6.01 us
    pallas_call x1, Pallas kernels, panel_weights(): pl.pallas_call(weights_kernel, grid=(panels // tile,), in_specs=[pl.Block...  5.48 us
    unnamed x11, local copies, waits for them, and re-layouts  4.86 us
  transfers between devices with their start and end apart: 4, of which 1 were waited for; matrix products, arithmetic and copies ran while one was open for 0% of the time, Pallas kernels for 66%

profile of v5, /device:TPU:0, one launch (start us, length us, event | category | flops | bytes accessed | tf_op | source)
XLA Modules:
  0.0 160.5 jit_solution(12949841184733785758)
XLA Ops:
  0.0 0.0 copy-start
  0.0 1.6 copy-done
  1.6 0.0 copy-start.1
  1.6 0.5 inverse_pack.5
  2.1 3.1 %collective-permute-start = (bf16[256,1024]{1,0:T(8,128)(2,1)S(1)}, bf16[256,1024]{1,0:T(8,128)(2,1)}, u32[]{:S(2)}, u32[]{:S(2)}) collective-permute-start(bf16[256,1024]{1,0:T(8,128)(2,1)S(1)} %inverse_pack.5), channel_id=1, source_target_pairs={{0,1},{1,2},{2,3},{3,0},{4,5},{5,6},{6,7},{7,4},{8,9},{9,10},{10,1... | collective-permute-start | bytes 1572872 | tf_op jit(solution)/shard_map/ppermute | solution.py:509
  5.1 0.0 copy-done.1
  5.1 0.5 inverse_pack.6
  5.6 0.0 copy-start.4
  5.6 2.7 %collective-permute-start.1 = (bf16[256,1024]{1,0:T(8,128)(2,1)S(1)}, bf16[256,1024]{1,0:T(8,128)(2,1)}, u32[]{:S(2)}, u32[]{:S(2)}) collective-permute-start(bf16[256,1024]{1,0:T(8,128)(2,1)S(1)} %inverse_pack.6), channel_id=1, source_target_pairs={{0,2},{1,3},{2,0},{3,1},{4,6},{5,7},{6,4},{7,5},{8,10},{9,11},{10,... | collective-permute-start | bytes 1572872 | tf_op jit(solution)/shard_map/ppermute | solution.py:509
  8.3 1.2 inverse_pack.7
  9.4 1.3 collective-permute-start.2
  10.8 0.5 inverse_pack.4.refs_0_
  11.3 0.0 copy-start.2
  11.3 0.8 copy-done.2
  12.1 0.0 copy-done.4
  12.1 0.8 copy.10
  12.9 28.8 %send_rows.1 = bf16[12288,128]{1,0:T(8,128)(2,1)} custom-call(s32[16384]{0:T(1024)} %bitcast.14, bf16[96,16384]{1,0:T(8,128)(2,1)} %source_ref.1), custom_call_target="tpu_custom_call" | custom-call | bytes 62914560 | tf_op jit(solution)/shard_map/send_rows/pallas_call | solution.py:124
  41.7 5.5 %panel_weights.1 = (f32[256,2048]{1,0:T(8,128)}, f32[256,2048]{1,0:T(8,128)}) custom-call(f32[3,2048]{1,0:T(4,128)} %points_ref.3, s32[1,2048]{1,0:T(1,128)} %bitcast.16, f32[256,3]{1,0:T(8,128)} %bitcast.13), custom_call_target="tpu_custom_call" | custom-call | flops 10485760 | bytes 4194304 | tf_op jit(solution)/shard_map/panel_weights/pallas_call | solution.py:228
  47.2 0.0 collective-permute-done.refs_1_
  47.2 0.0 collective-permute-done.1.refs_2_
  47.2 0.0 collective-permute-done.2.refs_3_
  47.2 9.6 %all-to-all-start = ((bf16[32,384,128]{2,1,0:T(8,128)(2,1)}), bf16[32,384,128]{2,1,0:T(8,128)(2,1)S(1)}, u32[]{:S(2)}, u32[]{:S(2)}) async-start(bf16[32,384,128]{2,1,0:T(8,128)(2,1)} %bitcast.12), calls=%async_computation | async-start | bytes 6291456 | tf_op jit(solution)/shard_map/all_to_all | solution.py:513
  56.8 6.0 %pair_products.1.products_ref = bf16[16384,128]{1,0:T(8,128)(2,1)} custom-call(s32[1]{0:T(128)} %bitcast.10.group_ref, bf16[256,1024]{1,0:T(8,128)(2,1)} %copy-done.2, bf16[256,1024]{1,0:T(8,128)(2,1)} %collective-permute-done.refs_1_, bf16[256,1024]{1,0:T(8,128)(2,1)} %collective-permute-done.1.refs_2_, bf16[256,1024]{1,0:T(8,128)(2,1)} %collective-permute-done.2.refs_3_), custom_call_target="tpu_custom_call" | custom-call | bytes 20971520 | tf_op jit(solution)/shard_map/pair_products/pallas_call | solution.py:342
  62.8 63.8 %blend.1.blend_ref = bf16[16384,2048]{1,0:T(8,128)(2,1)} custom-call(f32[3,2048]{1,0:T(4,128)} %points_ref.3, f32[256,2048]{1,0:T(8,128)} %get-tuple-element.21.five_ref, f32[256,2048]{1,0:T(8,128)} %get-tuple-element.22.four_ref, f32[3,16384]{1,0:T(4,128)} %support_ref.1), custom_call_target="tpu_custom_call" | custom-call | flops 2147483648 | bytes 134217728 | tf_op jit(solution)/shard_map/blend/pallas_call | solution.py:282
  126.6 0.3 all-to-all-done
  126.9 0.0 copy-start.3
  127.0 1.6 %copy-done.3 = bf16[32,384,128]{2,1,0:T(8,128)(2,1)} copy-done((bf16[32,384,128]{2,1,0:T(8,128)(2,1)}, bf16[32,384,128]{2,1,0:T(8,128)(2,1)S(1)}, u32[]{:S(2)}) %copy-start.3) | copy-done | bytes 3145752
  128.6 31.9 %moved_normals.1 = f32[32,2048]{1,0:T(8,128)} custom-call(s32[16384]{0:T(1024)} %bitcast.15, bf16[12288,128]{1,0:T(8,128)(2,1)} %bitcast.11, bf16[16384,128]{1,0:T(8,128)(2,1)} %pair_products.1.products_ref, bf16[16384,2048]{1,0:T(8,128)(2,1)} %blend.1.blend_ref, f32[3,2048]{1,0:T(4,128)} %normals_ref.1), custom_call_target="tpu_custom_call" | custom-call | flops 6442450944 | bytes 67108864 | tf_op jit(solution)/shard_map/moved_normals/pallas_call | solution.py:440
Async XLA Ops:
  0.0 1.6 copy-start
  1.6 3.6 %copy-start.1 = (bf16[16,64,1024]{2,1,0:T(8,128)(2,1)S(1)}, bf16[16,64,1024]{2,1,0:T(8,128)(2,1)}, u32[]{:S(2)}) copy-start(bf16[16,64,1024]{2,1,0:T(8,128)(2,1)} %inverse_ref.7) | copy-start | bytes 6291460
  2.1 45.1 %collective-permute-start = (bf16[256,1024]{1,0:T(8,128)(2,1)S(1)}, bf16[256,1024]{1,0:T(8,128)(2,1)}, u32[]{:S(2)}, u32[]{:S(2)}) collective-permute-start(bf16[256,1024]{1,0:T(8,128)(2,1)S(1)} %inverse_pack.5), channel_id=1, source_target_pairs={{0,1},{1,2},{2,3},{3,0},{4,5},{5,6},{6,7},{7,4},{8,9},{9,10},{10,1... | collective-permute-start | bytes 1572872 | tf_op jit(solution)/shard_map/ppermute | solution.py:509
  5.6 6.5 %copy-start.4 = (f32[3,256]{1,0:T(4,128)S(1)}, f32[3,256]{1,0:T(4,128)}, u32[]{:S(2)}) copy-start(f32[3,256]{1,0:T(4,128)} %param.16) | copy-start | bytes 9220
  5.6 41.6 %collective-permute-start.1 = (bf16[256,1024]{1,0:T(8,128)(2,1)S(1)}, bf16[256,1024]{1,0:T(8,128)(2,1)}, u32[]{:S(2)}, u32[]{:S(2)}) collective-permute-start(bf16[256,1024]{1,0:T(8,128)(2,1)S(1)} %inverse_pack.6), channel_id=1, source_target_pairs={{0,2},{1,3},{2,0},{3,1},{4,6},{5,7},{6,4},{7,5},{8,10},{9,11},{10,... | collective-permute-start | bytes 1572872 | tf_op jit(solution)/shard_map/ppermute | solution.py:509
  9.4 37.8 %collective-permute-start.2 = (bf16[256,1024]{1,0:T(8,128)(2,1)}, bf16[256,1024]{1,0:T(8,128)(2,1)}, u32[]{:S(2)}, u32[]{:S(2)}) collective-permute-start(bf16[256,1024]{1,0:T(8,128)(2,1)} %inverse_pack.7), channel_id=1, source_target_pairs={{0,3},{1,0},{2,1},{3,2},{4,7},{5,4},{6,5},{7,6},{8,11},{9,8},{10,9... | collective-permute-start | bytes 1572872 | tf_op jit(solution)/shard_map/ppermute | solution.py:509
  11.3 0.8 copy-start.2
  47.2 79.7 %all-to-all-start = ((bf16[32,384,128]{2,1,0:T(8,128)(2,1)}), bf16[32,384,128]{2,1,0:T(8,128)(2,1)S(1)}, u32[]{:S(2)}, u32[]{:S(2)}) async-start(bf16[32,384,128]{2,1,0:T(8,128)(2,1)} %bitcast.12), calls=%async_computation | async-start | bytes 6291456 | tf_op jit(solution)/shard_map/all_to_all | solution.py:513
  126.9 1.6 %copy-start.3 = (bf16[32,384,128]{2,1,0:T(8,128)(2,1)}, bf16[32,384,128]{2,1,0:T(8,128)(2,1)S(1)}, u32[]{:S(2)}) copy-start(bf16[32,384,128]{2,1,0:T(8,128)(2,1)S(1)} %all-to-all-done) | copy-start | bytes 9437188

commit v6 on v5

--- a/solution.py
+++ b/solution.py
@@ -143,7 +143,8 @@
     )(index, displacement)
 
 
-def unpack_rows(per, packed_ref, rows_ref, first, end):
+def unpack_rows(per, packed_ref, rows_ref):
+    peers = rows_ref.shape[0] // per
     quarter = per // 4
     lane = lax.broadcasted_iota(jnp.int32, (quarter, LANES), 1)
 
@@ -160,7 +161,7 @@
         rows_ref[pl.ds(to, quarter), :] = last
         return carry
 
-    lax.fori_loop(first, end, peer, 0)
+    lax.fori_loop(0, peers, peer, 0)
 
 
 def splits(x):
@@ -355,9 +356,9 @@
     )(group.reshape(1), *inverses)
 
 
-def moved_kernel(modes, per, index_ref, source_ref, products_ref, blend_ref, normals_ref, *refs):
+def moved_kernel(modes, per, index_ref, packed_ref, products_ref, blend_ref, normals_ref, *refs):
     out_ref, rows_ref, picked_ref, values_ref, coef_ref, summed_ref = refs[:6]
-    total_ref, blend_slots, arrived, packed_ref, landed = refs[6:]
+    total_ref, blend_slots, arrived = refs[6:]
     step = pl.program_id(0)
     steps = pl.num_programs(0) - 2
     block = picked_ref.shape[0]
@@ -372,53 +373,52 @@
 
     @pl.when(step == 0)
     def _():
-        rows = packed_ref.shape[0] // PIECES
-        pieces = []
-        for i in range(PIECES):
-            span = pl.ds(i * rows, rows)
-            pieces.append(
-                pltpu.make_async_copy(source_ref.at[span], packed_ref.at[span], landed.at[i])
-            )
-            pieces[i].start()
         for b in range(depth):
             fetch(b).start()
         total_ref[...] = jnp.zeros_like(total_ref)
         values_ref[...] = jnp.zeros_like(values_ref)
-        coef_ref[...] = jnp.zeros_like(coef_ref)
-        peers = rows_ref.shape[0] // (per * PIECES)
-        for i in range(PIECES):
-            pieces[i].wait()
-            unpack_rows(per, packed_ref, rows_ref, i * peers, (i + 1) * peers)
-        fetch(0).wait()
-
-    @pl.when(step >= 3)
+        unpack_rows(per, packed_ref, rows_ref)
+
+    @pl.when(step >= 2)
     def _():
         fetch(step - 2).wait()
 
-        @pl.when(step - 3 + depth < steps)
+        @pl.when(jnp.logical_and(step >= 3, step - 3 + depth < steps))
         def _():
             fetch(step - 3 + depth).start()
 
-    summed_ref[...] = coef_ref[...]
     slot = lax.rem(jnp.maximum(step - 2, 0), depth)
     base = jnp.minimum(step, steps - 1) * block
     pairs = block // LANES
     tile = total_ref.shape[1] // pairs
-    for pair in range(pairs):
-        columns = slice(pair * tile, (pair + 1) * tile)
-        total_ref[:, columns] += jnp.dot(
-            summed_ref[...], blend_slots[slot, :, columns], preferred_element_type=jnp.float32
-        )
-        for r in range(pair * LANES, (pair + 1) * LANES):
-            picked_ref[r : r + 1, :] = rows_ref[pl.ds(index_ref[base + r], 1), :]
-        at = pair * LANES
-        coef = jnp.dot(
-            products_ref[at : at + LANES, :],
-            values_ref[at : at + LANES, :],
-            preferred_element_type=jnp.float32,
-        )
-        coef_ref[:, at : at + LANES] = coef.T[: 3 * modes].astype(jnp.bfloat16)
-    values_ref[...] = picked_ref[...].astype(jnp.bfloat16)
+
+    def stages(summing, picking):
+        if summing:
+            summed_ref[...] = coef_ref[...]
+        for pair in range(pairs):
+            columns = slice(pair * tile, (pair + 1) * tile)
+            if summing:
+                total_ref[:, columns] += jnp.dot(
+                    summed_ref[...],
+                    blend_slots[slot, :, columns],
+                    preferred_element_type=jnp.float32,
+                )
+            at = pair * LANES
+            if picking:
+                for r in range(at, at + LANES):
+                    picked_ref[r : r + 1, :] = rows_ref[pl.ds(index_ref[base + r], 1), :]
+            coef = jnp.dot(
+                products_ref[at : at + LANES, :],
+                values_ref[at : at + LANES, :],
+                preferred_element_type=jnp.float32,
+            )
+            coef_ref[:, at : at + LANES] = coef.T[: 3 * modes].astype(jnp.bfloat16)
+        if picking:
+            values_ref[...] = picked_ref[...].astype(jnp.bfloat16)
+
+    pl.when(step < 2)(lambda: stages(False, True))
+    pl.when(jnp.logical_and(step >= 2, step < steps))(lambda: stages(True, True))
+    pl.when(step >= steps)(lambda: stages(True, False))
 
     @pl.when(step == steps + 1)
     def _():
@@ -442,7 +442,7 @@
         grid=(steps + 2,),
         in_specs=[
             pl.BlockSpec(memory_space=pltpu.SMEM),
-            pl.BlockSpec(memory_space=pl.ANY),
+            pl.BlockSpec(memory_space=pltpu.VMEM),
             pl.BlockSpec((block, LANES), lambda i: (before(i), 0)),
             pl.BlockSpec(memory_space=pl.ANY),
             pl.BlockSpec((3, panels), lambda i: (0, 0)),
@@ -458,10 +458,8 @@
             pltpu.VMEM((3 * modes, panels), jnp.float32),
             pltpu.VMEM((BLEND_DEPTH, block, panels), jnp.bfloat16),
             pltpu.SemaphoreType.DMA((BLEND_DEPTH,)),
-            pltpu.VMEM(packed.shape, jnp.bfloat16),
-            pltpu.SemaphoreType.DMA((PIECES,)),
-        ],
-        compiler_params=params(60),
+        ],
+        compiler_params=params(34),
         cost_estimate=pl.CostEstimate(
             flops=2 * 3 * modes * panels * slots,
             bytes_accessed=2 * panels * slots,

time: 161 us -> 157 us (0.975)
  Pallas kernels: 139 us -> 134 us
    pallas_call x1, Pallas kernels: 31.9 us -> 27.5 us  [moved_normals(): pl.pallas_call(functools.partial(moved_kernel, modes, per), grid=(steps +...]
    unnamed x11 -> x15, local copies, waits for them, and re-layouts: 4.86 us -> 5.4 us
  transfers between devices with their start and end apart: 4 -> 4, of which waited for: 1 -> 1; matrix products, arithmetic and copies ran while one was open for 0% -> 1% of each run, Pallas kernels for 66% -> 68%
where the time goes in v6:
time: 157 us
  Pallas kernels  134 us (85%)
  starting transfers between devices  16.6 us (11%)
  local copies, waits for them, and re-layouts  5.4 us (3%)
    pallas_call x1, Pallas kernels, blend_entry_major(): pl.pallas_call(functools.partial(blend_kernel, support_count), grid=(slot...  63.8 us
    pallas_call x1, Pallas kernels, send_rows(): pl.pallas_call(functools.partial(send_kernel, per), in_specs=[pl.BlockSpe...  28.8 us
    pallas_call x1, Pallas kernels, moved_normals(): pl.pallas_call(functools.partial(moved_kernel, modes, per), grid=(steps +...  27.5 us
    all_to_all x1, starting transfers between devices, shards(): lax.all_to_all(outgoing.reshape(devices, per * 3 // 4, LANES), axes, 0, 0...  9.54 us
    ppermute x3, starting transfers between devices, shards(): inverses.append(lax.ppermute(packs[k], 'group', ring))  7.08 us
    pallas_call x1, Pallas kernels, pair_products(): pl.pallas_call(functools.partial(products_kernel, support_count, groups),...  6 us
    pallas_call x1, Pallas kernels, panel_weights(): pl.pallas_call(weights_kernel, grid=(panels // tile,), in_specs=[pl.Block...  5.54 us
    unnamed x15, local copies, waits for them, and re-layouts  5.4 us
  transfers between devices with their start and end apart: 4, of which 1 were waited for; matrix products, arithmetic and copies ran while one was open for 1% of the time, Pallas kernels for 68%

profile of v6, /device:TPU:0, one launch (start us, length us, event | category | flops | bytes accessed | tf_op | source)
XLA Modules:
  0.0 156.6 jit_solution(515710120201902808)
XLA Ops:
  0.0 0.0 copy-start
  0.0 1.6 %copy-done = bf16[16,64,1024]{2,1,0:T(8,128)(2,1)S(1)} copy-done((bf16[16,64,1024]{2,1,0:T(8,128)(2,1)S(1)}, bf16[16,64,1024]{2,1,0:T(8,128)(2,1)}, u32[]{:S(2)}) %copy-start) | copy-done | bytes 2097176
  1.6 0.0 copy-start.1
  1.6 0.5 inverse_pack.5
  2.1 3.1 %collective-permute-start = (bf16[256,1024]{1,0:T(8,128)(2,1)S(1)}, bf16[256,1024]{1,0:T(8,128)(2,1)}, u32[]{:S(2)}, u32[]{:S(2)}) collective-permute-start(bf16[256,1024]{1,0:T(8,128)(2,1)S(1)} %inverse_pack.5), channel_id=1, source_target_pairs={{0,1},{1,2},{2,3},{3,0},{4,5},{5,6},{6,7},{7,4},{8,9},{9,10},{10,1... | collective-permute-start | bytes 1572872 | tf_op jit(solution)/shard_map/ppermute | solution.py:507
  5.1 0.0 copy-done.1
  5.1 0.5 inverse_pack.6
  5.6 0.0 copy-start.6
  5.6 2.7 %collective-permute-start.1 = (bf16[256,1024]{1,0:T(8,128)(2,1)S(1)}, bf16[256,1024]{1,0:T(8,128)(2,1)}, u32[]{:S(2)}, u32[]{:S(2)}) collective-permute-start(bf16[256,1024]{1,0:T(8,128)(2,1)S(1)} %inverse_pack.6), channel_id=1, source_target_pairs={{0,2},{1,3},{2,0},{3,1},{4,6},{5,7},{6,4},{7,5},{8,10},{9,11},{10,... | collective-permute-start | bytes 1572872 | tf_op jit(solution)/shard_map/ppermute | solution.py:507
  8.3 1.2 inverse_pack.7
  9.4 1.3 collective-permute-start.2
  10.8 0.5 inverse_pack.4.refs_0_
  11.3 0.0 copy-start.3
  11.3 0.8 copy-done.3
  12.1 0.0 copy-done.6
  12.1 0.8 copy.10
  12.9 28.8 %send_rows.1 = bf16[12288,128]{1,0:T(8,128)(2,1)} custom-call(s32[16384]{0:T(1024)} %bitcast.15, bf16[96,16384]{1,0:T(8,128)(2,1)} %source_ref.1), custom_call_target="tpu_custom_call" | custom-call | bytes 62914560 | tf_op jit(solution)/shard_map/send_rows/pallas_call | solution.py:124
  41.7 5.5 %panel_weights.1 = (f32[256,2048]{1,0:T(8,128)}, f32[256,2048]{1,0:T(8,128)}) custom-call(f32[3,2048]{1,0:T(4,128)} %points_ref.3, s32[1,2048]{1,0:T(1,128)} %bitcast.16, f32[256,3]{1,0:T(8,128)} %bitcast.14), custom_call_target="tpu_custom_call" | custom-call | flops 10485760 | bytes 4194304 | tf_op jit(solution)/shard_map/panel_weights/pallas_call | solution.py:229
  47.2 0.0 collective-permute-done.refs_1_
  47.2 0.0 collective-permute-done.1.refs_2_
  47.2 0.0 collective-permute-done.2.refs_3_
  47.2 9.5 %all-to-all-start = ((bf16[32,384,128]{2,1,0:T(8,128)(2,1)}), bf16[32,384,128]{2,1,0:T(8,128)(2,1)S(1)}, u32[]{:S(2)}, u32[]{:S(2)}) async-start(bf16[32,384,128]{2,1,0:T(8,128)(2,1)} %bitcast.13), calls=%async_computation | async-start | bytes 6291456 | tf_op jit(solution)/shard_map/all_to_all | solution.py:511
  56.8 6.0 %pair_products.1.products_ref = bf16[16384,128]{1,0:T(8,128)(2,1)} custom-call(s32[1]{0:T(128)} %bitcast.10.group_ref, bf16[256,1024]{1,0:T(8,128)(2,1)} %copy-done.3, bf16[256,1024]{1,0:T(8,128)(2,1)} %collective-permute-done.refs_1_, bf16[256,1024]{1,0:T(8,128)(2,1)} %collective-permute-done.1.refs_2_, bf16[256,1024]{1,0:T(8,128)(2,1)} %collective-permute-done.2.refs_3_), custom_call_target="tpu_custom_call" | custom-call | bytes 20971520 | tf_op jit(solution)/shard_map/pair_products/pallas_call | solution.py:343
  62.8 0.0 copy-start.4
  62.8 0.0 copy-start.5
  62.8 63.8 %blend.1.blend_ref = bf16[16384,2048]{1,0:T(8,128)(2,1)} custom-call(f32[3,2048]{1,0:T(4,128)} %points_ref.3, f32[256,2048]{1,0:T(8,128)} %get-tuple-element.21.five_ref, f32[256,2048]{1,0:T(8,128)} %get-tuple-element.22.four_ref, f32[3,16384]{1,0:T(4,128)} %support_ref.1), custom_call_target="tpu_custom_call" | custom-call | flops 2147483648 | bytes 134217728 | tf_op jit(solution)/shard_map/blend/pallas_call | solution.py:283
  126.6 0.3 all-to-all-done
  126.9 0.0 copy-done.4
  127.0 0.0 copy-done.5
  127.0 0.0 copy-start.2
  127.0 2.2 %copy-done.2 = bf16[16384,128]{1,0:T(8,128)(2,1)S(1)} copy-done((bf16[16384,128]{1,0:T(8,128)(2,1)S(1)}, bf16[16384,128]{1,0:T(8,128)(2,1)}, u32[]{:S(2)}) %copy-start.2) | copy-done | bytes 4194328
  129.1 27.5 %moved_normals.1 = f32[32,2048]{1,0:T(8,128)} custom-call(s32[16384]{0:T(1024)S(1)} %bitcast.12, bf16[12288,128]{1,0:T(8,128)(2,1)S(1)} %bitcast.11, bf16[16384,128]{1,0:T(8,128)(2,1)S(1)} %copy-done.2, bf16[16384,2048]{1,0:T(8,128)(2,1)} %blend.1.blend_ref, f32[3,2048]{1,0:T(4,128)S(1)} %copy-done.5), custom_call_target="tpu_custom_call" | custom-call | flops 6442450944 | bytes 67108864 | tf_op jit(solution)/shard_map/moved_normals/pallas_call | solution.py:440
Async XLA Ops:
  0.0 1.6 %copy-start = (bf16[16,64,1024]{2,1,0:T(8,128)(2,1)S(1)}, bf16[16,64,1024]{2,1,0:T(8,128)(2,1)}, u32[]{:S(2)}) copy-start(bf16[16,64,1024]{2,1,0:T(8,128)(2,1)} %inverse_ref.7) | copy-start | bytes 6291460
  1.6 3.6 %copy-start.1 = (bf16[16,64,1024]{2,1,0:T(8,128)(2,1)S(1)}, bf16[16,64,1024]{2,1,0:T(8,128)(2,1)}, u32[]{:S(2)}) copy-start(bf16[16,64,1024]{2,1,0:T(8,128)(2,1)} %inverse_ref.7) | copy-start | bytes 6291460
  2.1 45.2 %collective-permute-start = (bf16[256,1024]{1,0:T(8,128)(2,1)S(1)}, bf16[256,1024]{1,0:T(8,128)(2,1)}, u32[]{:S(2)}, u32[]{:S(2)}) collective-permute-start(bf16[256,1024]{1,0:T(8,128)(2,1)S(1)} %inverse_pack.5), channel_id=1, source_target_pairs={{0,1},{1,2},{2,3},{3,0},{4,5},{5,6},{6,7},{7,4},{8,9},{9,10},{10,1... | collective-permute-start | bytes 1572872 | tf_op jit(solution)/shard_map/ppermute | solution.py:507
  5.6 6.5 %copy-start.6 = (f32[3,256]{1,0:T(4,128)S(1)}, f32[3,256]{1,0:T(4,128)}, u32[]{:S(2)}) copy-start(f32[3,256]{1,0:T(4,128)} %param.16) | copy-start | bytes 9220
  5.6 41.6 %collective-permute-start.1 = (bf16[256,1024]{1,0:T(8,128)(2,1)S(1)}, bf16[256,1024]{1,0:T(8,128)(2,1)}, u32[]{:S(2)}, u32[]{:S(2)}) collective-permute-start(bf16[256,1024]{1,0:T(8,128)(2,1)S(1)} %inverse_pack.6), channel_id=1, source_target_pairs={{0,2},{1,3},{2,0},{3,1},{4,6},{5,7},{6,4},{7,5},{8,10},{9,11},{10,... | collective-permute-start | bytes 1572872 | tf_op jit(solution)/shard_map/ppermute | solution.py:507
  9.4 37.8 %collective-permute-start.2 = (bf16[256,1024]{1,0:T(8,128)(2,1)}, bf16[256,1024]{1,0:T(8,128)(2,1)}, u32[]{:S(2)}, u32[]{:S(2)}) collective-permute-start(bf16[256,1024]{1,0:T(8,128)(2,1)} %inverse_pack.7), channel_id=1, source_target_pairs={{0,3},{1,0},{2,1},{3,2},{4,7},{5,4},{6,5},{7,6},{8,11},{9,8},{10,9... | collective-permute-start | bytes 1572872 | tf_op jit(solution)/shard_map/ppermute | solution.py:507
  11.3 0.8 copy-start.3
  47.2 79.7 %all-to-all-start = ((bf16[32,384,128]{2,1,0:T(8,128)(2,1)}), bf16[32,384,128]{2,1,0:T(8,128)(2,1)S(1)}, u32[]{:S(2)}, u32[]{:S(2)}) async-start(bf16[32,384,128]{2,1,0:T(8,128)(2,1)} %bitcast.13), calls=%async_computation | async-start | bytes 6291456 | tf_op jit(solution)/shard_map/all_to_all | solution.py:511
  62.8 64.2 %copy-start.4 = (s32[1,16384]{1,0:T(1,128)S(1)}, s32[1,16384]{1,0:T(1,128)}, u32[]{:S(2)}) copy-start(s32[1,16384]{1,0:T(1,128)} %param.11) | copy-start | bytes 196612
  62.8 64.2 %copy-start.5 = (f32[3,2048]{1,0:T(4,128)S(1)}, f32[3,2048]{1,0:T(4,128)}, u32[]{:S(2)}) copy-start(f32[3,2048]{1,0:T(4,128)} %normals_ref.1) | copy-start | bytes 73732
  127.0 2.2 %copy-start.2 = (bf16[16384,128]{1,0:T(8,128)(2,1)S(1)}, bf16[16384,128]{1,0:T(8,128)(2,1)}, u32[]{:S(2)}) copy-start(bf16[16384,128]{1,0:T(8,128)(2,1)} %pair_products.1.products_ref) | copy-start | bytes 12582916

commit v7 on v6

--- a/solution.py
+++ b/solution.py
@@ -279,14 +279,14 @@
 def blend_entry_major(points, weights, support_xyz, support_count):
     panels = points.shape[1]
     slots = support_xyz.shape[1]
-    block = 8 * support_count
+    block = 16 * support_count
     return pl.pallas_call(
         functools.partial(blend_kernel, support_count),
         grid=(slots // block,),
         in_specs=[
             pl.BlockSpec((3, panels), lambda i: (0, 0)),
-            pl.BlockSpec((8, panels), lambda i: (i, 0)),
-            pl.BlockSpec((8, panels), lambda i: (i, 0)),
+            pl.BlockSpec((16, panels), lambda i: (i, 0)),
+            pl.BlockSpec((16, panels), lambda i: (i, 0)),
             pl.BlockSpec((3, block), lambda i: (0, i)),
         ],
         out_specs=pl.BlockSpec((block, panels), lambda i: (i, 0)),
@@ -306,7 +306,7 @@
 
 BLOCK_PATCHES = 16
 BLEND_DEPTH = 4
-PRODUCT_PATCHES = 64
+PRODUCT_PATCHES = 128
 
 
 def products_kernel(support_count, groups, group_ref, *refs):
@@ -347,7 +347,7 @@
         + [pl.BlockSpec((PRODUCT_PATCHES, width), lambda i: (i, 0))] * groups,
         out_specs=pl.BlockSpec((block, LANES), lambda i: (i, 0)),
         out_shape=jax.ShapeDtypeStruct((patches * support_count, LANES), jnp.bfloat16),
-        scratch_shapes=[pltpu.VMEM((block // 2, LANES), jnp.float32)],
+        scratch_shapes=[pltpu.VMEM((block // 2 + LANES, LANES), jnp.float32)],
         compiler_params=params(60),
         cost_estimate=pl.CostEstimate(
             flops=0, bytes_accessed=20 * MIB, transcendentals=0

time: 157 us -> 157 us (level)
  Pallas kernels: 134 us -> 132 us
  waiting for transfers between devices: 0.33 us -> 2.07 us
    pallas_call x1, Pallas kernels: 63.8 us -> 61.9 us  [blend_entry_major(): pl.pallas_call(functools.partial(blend_kernel, support_count), grid=(slot...]
    all_to_all x1, waiting for transfers between devices: 0.32 us -> 2.06 us  [shards(): lax.all_to_all(outgoing.reshape(devices, per * 3 // 4, LANES), axes, 0, 0...]
  transfers between devices with their start and end apart: 4 -> 4, of which waited for: 1 -> 1; matrix products, arithmetic and copies ran while one was open for 1% -> 1% of each run, Pallas kernels for 68% -> 67%
where the time goes in v7:
time: 157 us
  Pallas kernels  132 us (84%)
  starting transfers between devices  16.6 us (11%)
  local copies, waits for them, and re-layouts  5.4 us (3%)
  waiting for transfers between devices  2.07 us (1%)
    pallas_call x1, Pallas kernels, blend_entry_major(): pl.pallas_call(functools.partial(blend_kernel, support_count), grid=(slot...  61.9 us
    pallas_call x1, Pallas kernels, send_rows(): pl.pallas_call(functools.partial(send_kernel, per), in_specs=[pl.BlockSpe...  28.8 us
    pallas_call x1, Pallas kernels, moved_normals(): pl.pallas_call(functools.partial(moved_kernel, modes, per), grid=(steps +...  27.5 us
    all_to_all x1, starting transfers between devices, shards(): lax.all_to_all(outgoing.reshape(devices, per * 3 // 4, LANES), axes, 0, 0...  9.54 us
    ppermute x3, starting transfers between devices, shards(): inverses.append(lax.ppermute(packs[k], 'group', ring))  7.08 us
    pallas_call x1, Pallas kernels, pair_products(): pl.pallas_call(functools.partial(products_kernel, support_count, groups),...  6.18 us
    pallas_call x1, Pallas kernels, panel_weights(): pl.pallas_call(weights_kernel, grid=(panels // tile,), in_specs=[pl.Block...  5.54 us
    unnamed x15, local copies, waits for them, and re-layouts  5.4 us
  transfers between devices with their start and end apart: 4, of which 1 were waited for; matrix products, arithmetic and copies ran while one was open for 1% of the time, Pallas kernels for 67%

profile of v7, /device:TPU:0, one launch (start us, length us, event | category | flops | bytes accessed | tf_op | source)
XLA Modules:
  0.0 156.6 jit_solution(13699364920690591088)
XLA Ops:
  0.0 0.0 copy-start
  0.0 1.6 %copy-done = bf16[16,64,1024]{2,1,0:T(8,128)(2,1)S(1)} copy-done((bf16[16,64,1024]{2,1,0:T(8,128)(2,1)S(1)}, bf16[16,64,1024]{2,1,0:T(8,128)(2,1)}, u32[]{:S(2)}) %copy-start) | copy-done | bytes 2097176
  1.6 0.0 copy-start.1
  1.6 0.5 inverse_pack.5
  2.1 3.1 %collective-permute-start = (bf16[256,1024]{1,0:T(8,128)(2,1)S(1)}, bf16[256,1024]{1,0:T(8,128)(2,1)}, u32[]{:S(2)}, u32[]{:S(2)}) collective-permute-start(bf16[256,1024]{1,0:T(8,128)(2,1)S(1)} %inverse_pack.5), channel_id=1, source_target_pairs={{0,1},{1,2},{2,3},{3,0},{4,5},{5,6},{6,7},{7,4},{8,9},{9,10},{10,1... | collective-permute-start | bytes 1572872 | tf_op jit(solution)/shard_map/ppermute | solution.py:507
  5.1 0.0 copy-done.1
  5.1 0.5 inverse_pack.6
  5.6 0.0 copy-start.6
  5.6 2.7 %collective-permute-start.1 = (bf16[256,1024]{1,0:T(8,128)(2,1)S(1)}, bf16[256,1024]{1,0:T(8,128)(2,1)}, u32[]{:S(2)}, u32[]{:S(2)}) collective-permute-start(bf16[256,1024]{1,0:T(8,128)(2,1)S(1)} %inverse_pack.6), channel_id=1, source_target_pairs={{0,2},{1,3},{2,0},{3,1},{4,6},{5,7},{6,4},{7,5},{8,10},{9,11},{10,... | collective-permute-start | bytes 1572872 | tf_op jit(solution)/shard_map/ppermute | solution.py:507
  8.3 1.2 inverse_pack.7
  9.4 1.3 collective-permute-start.2
  10.8 0.5 inverse_pack.4.refs_0_
  11.3 0.0 copy-start.3
  11.3 0.8 copy-done.3
  12.1 0.0 copy-done.6
  12.1 0.8 copy.10
  12.9 28.8 %send_rows.1 = bf16[12288,128]{1,0:T(8,128)(2,1)} custom-call(s32[16384]{0:T(1024)} %bitcast.15, bf16[96,16384]{1,0:T(8,128)(2,1)} %source_ref.1), custom_call_target="tpu_custom_call" | custom-call | bytes 62914560 | tf_op jit(solution)/shard_map/send_rows/pallas_call | solution.py:124
  41.7 5.5 %panel_weights.1 = (f32[256,2048]{1,0:T(8,128)}, f32[256,2048]{1,0:T(8,128)}) custom-call(f32[3,2048]{1,0:T(4,128)} %points_ref.3, s32[1,2048]{1,0:T(1,128)} %bitcast.16, f32[256,3]{1,0:T(8,128)} %bitcast.14), custom_call_target="tpu_custom_call" | custom-call | flops 10485760 | bytes 4194304 | tf_op jit(solution)/shard_map/panel_weights/pallas_call | solution.py:229
  47.2 0.0 collective-permute-done.refs_1_
  47.2 0.0 collective-permute-done.1.refs_2_
  47.2 0.0 collective-permute-done.2.refs_3_
  47.2 9.5 %all-to-all-start = ((bf16[32,384,128]{2,1,0:T(8,128)(2,1)}), bf16[32,384,128]{2,1,0:T(8,128)(2,1)S(1)}, u32[]{:S(2)}, u32[]{:S(2)}) async-start(bf16[32,384,128]{2,1,0:T(8,128)(2,1)} %bitcast.13), calls=%async_computation | async-start | bytes 6291456 | tf_op jit(solution)/shard_map/all_to_all | solution.py:511
  56.8 6.2 %pair_products.1.products_ref = bf16[16384,128]{1,0:T(8,128)(2,1)} custom-call(s32[1]{0:T(128)} %bitcast.10.group_ref, bf16[256,1024]{1,0:T(8,128)(2,1)} %copy-done.3, bf16[256,1024]{1,0:T(8,128)(2,1)} %collective-permute-done.refs_1_, bf16[256,1024]{1,0:T(8,128)(2,1)} %collective-permute-done.1.refs_2_, bf16[256,1024]{1,0:T(8,128)(2,1)} %collective-permute-done.2.refs_3_), custom_call_target="tpu_custom_call" | custom-call | bytes 20971520 | tf_op jit(solution)/shard_map/pair_products/pallas_call | solution.py:343
  63.0 0.0 copy-start.4
  63.0 0.0 copy-start.5
  63.0 61.9 %blend.1.blend_ref = bf16[16384,2048]{1,0:T(8,128)(2,1)} custom-call(f32[3,2048]{1,0:T(4,128)} %points_ref.3, f32[256,2048]{1,0:T(8,128)} %get-tuple-element.21.five_ref, f32[256,2048]{1,0:T(8,128)} %get-tuple-element.22.four_ref, f32[3,16384]{1,0:T(4,128)} %support_ref.1), custom_call_target="tpu_custom_call" | custom-call | flops 2147483648 | bytes 134217728 | tf_op jit(solution)/shard_map/blend/pallas_call | solution.py:283
  124.9 2.1 %all-to-all-done = bf16[32,384,128]{2,1,0:T(8,128)(2,1)S(1)} async-done(((bf16[32,384,128]{2,1,0:T(8,128)(2,1)}), bf16[32,384,128]{2,1,0:T(8,128)(2,1)S(1)}, u32[]{:S(2)}, u32[]{:S(2)}) %all-to-all-start) | async-done | bytes 3145760 | tf_op jit(solution)/shard_map/all_to_all | solution.py:511
  126.9 0.0 copy-done.4
  127.0 0.0 copy-done.5
  127.0 0.0 copy-start.2
  127.0 2.2 %copy-done.2 = bf16[16384,128]{1,0:T(8,128)(2,1)S(1)} copy-done((bf16[16384,128]{1,0:T(8,128)(2,1)S(1)}, bf16[16384,128]{1,0:T(8,128)(2,1)}, u32[]{:S(2)}) %copy-start.2) | copy-done | bytes 4194328
  129.1 27.5 %moved_normals.1 = f32[32,2048]{1,0:T(8,128)} custom-call(s32[16384]{0:T(1024)S(1)} %bitcast.12, bf16[12288,128]{1,0:T(8,128)(2,1)S(1)} %bitcast.11, bf16[16384,128]{1,0:T(8,128)(2,1)S(1)} %copy-done.2, bf16[16384,2048]{1,0:T(8,128)(2,1)} %blend.1.blend_ref, f32[3,2048]{1,0:T(4,128)S(1)} %copy-done.5), custom_call_target="tpu_custom_call" | custom-call | flops 6442450944 | bytes 67108864 | tf_op jit(solution)/shard_map/moved_normals/pallas_call | solution.py:440
Async XLA Ops:
  0.0 1.6 %copy-start = (bf16[16,64,1024]{2,1,0:T(8,128)(2,1)S(1)}, bf16[16,64,1024]{2,1,0:T(8,128)(2,1)}, u32[]{:S(2)}) copy-start(bf16[16,64,1024]{2,1,0:T(8,128)(2,1)} %inverse_ref.7) | copy-start | bytes 6291460
  1.6 3.6 %copy-start.1 = (bf16[16,64,1024]{2,1,0:T(8,128)(2,1)S(1)}, bf16[16,64,1024]{2,1,0:T(8,128)(2,1)}, u32[]{:S(2)}) copy-start(bf16[16,64,1024]{2,1,0:T(8,128)(2,1)} %inverse_ref.7) | copy-start | bytes 6291460
  2.1 45.2 %collective-permute-start = (bf16[256,1024]{1,0:T(8,128)(2,1)S(1)}, bf16[256,1024]{1,0:T(8,128)(2,1)}, u32[]{:S(2)}, u32[]{:S(2)}) collective-permute-start(bf16[256,1024]{1,0:T(8,128)(2,1)S(1)} %inverse_pack.5), channel_id=1, source_target_pairs={{0,1},{1,2},{2,3},{3,0},{4,5},{5,6},{6,7},{7,4},{8,9},{9,10},{10,1... | collective-permute-start | bytes 1572872 | tf_op jit(solution)/shard_map/ppermute | solution.py:507
  5.6 6.5 %copy-start.6 = (f32[3,256]{1,0:T(4,128)S(1)}, f32[3,256]{1,0:T(4,128)}, u32[]{:S(2)}) copy-start(f32[3,256]{1,0:T(4,128)} %param.16) | copy-start | bytes 9220
  5.6 41.6 %collective-permute-start.1 = (bf16[256,1024]{1,0:T(8,128)(2,1)S(1)}, bf16[256,1024]{1,0:T(8,128)(2,1)}, u32[]{:S(2)}, u32[]{:S(2)}) collective-permute-start(bf16[256,1024]{1,0:T(8,128)(2,1)S(1)} %inverse_pack.6), channel_id=1, source_target_pairs={{0,2},{1,3},{2,0},{3,1},{4,6},{5,7},{6,4},{7,5},{8,10},{9,11},{10,... | collective-permute-start | bytes 1572872 | tf_op jit(solution)/shard_map/ppermute | solution.py:507
  9.4 37.8 %collective-permute-start.2 = (bf16[256,1024]{1,0:T(8,128)(2,1)}, bf16[256,1024]{1,0:T(8,128)(2,1)}, u32[]{:S(2)}, u32[]{:S(2)}) collective-permute-start(bf16[256,1024]{1,0:T(8,128)(2,1)} %inverse_pack.7), channel_id=1, source_target_pairs={{0,3},{1,0},{2,1},{3,2},{4,7},{5,4},{6,5},{7,6},{8,11},{9,8},{10,9... | collective-permute-start | bytes 1572872 | tf_op jit(solution)/shard_map/ppermute | solution.py:507
  11.3 0.8 copy-start.3
  47.2 79.7 %all-to-all-start = ((bf16[32,384,128]{2,1,0:T(8,128)(2,1)}), bf16[32,384,128]{2,1,0:T(8,128)(2,1)S(1)}, u32[]{:S(2)}, u32[]{:S(2)}) async-start(bf16[32,384,128]{2,1,0:T(8,128)(2,1)} %bitcast.13), calls=%async_computation | async-start | bytes 6291456 | tf_op jit(solution)/shard_map/all_to_all | solution.py:511
  63.0 64.0 %copy-start.4 = (s32[1,16384]{1,0:T(1,128)S(1)}, s32[1,16384]{1,0:T(1,128)}, u32[]{:S(2)}) copy-start(s32[1,16384]{1,0:T(1,128)} %param.11) | copy-start | bytes 196612
  63.0 64.0 %copy-start.5 = (f32[3,2048]{1,0:T(4,128)S(1)}, f32[3,2048]{1,0:T(4,128)}, u32[]{:S(2)}) copy-start(f32[3,2048]{1,0:T(4,128)} %normals_ref.1) | copy-start | bytes 73732
  127.0 2.2 %copy-start.2 = (bf16[16384,128]{1,0:T(8,128)(2,1)S(1)}, bf16[16384,128]{1,0:T(8,128)(2,1)}, u32[]{:S(2)}) copy-start(bf16[16384,128]{1,0:T(8,128)(2,1)} %pair_products.1.products_ref) | copy-start | bytes 12582916
